TPU v7x, 128 devices: a whole 4x4x4 slice. The times are simulated.
128 devices in a mesh: grp: 4 (over x_lo, core), wide: 32 (over y, x_hi, z).
Axes of the slice: x: 4 (x_hi: 2, x_lo: 2; x = x_hi * 2 + x_lo), y: 4, z: 4, core: 2. Of those that a mesh axis runs over, the one named last changes fastest.
Arguments:
- token_ids: int32 [4, 8192], P('grp', 'wide'), may hold values from 0 to 49151
- targets: int32 [4, 8192], P('grp', 'wide'), may hold values from 0 to 49151
- segment_ids: int32 [4, 8192], P('grp', 'wide'), may hold values from 0 to 127, never falling along the last dimension, each value on 1 to 128 neighbouring positions
- row_counts: int32 [4, 32, 3], P('grp', 'wide'), may hold values from 0 to 1, as said below
- embed_table_master: float32 [4, 49152, 576], P('grp', 'wide')
- embed_table_first: float32 [4, 49152, 576], P('grp', 'wide'), may hold values from -2.861023e-06 to 2.861023e-06
- embed_table_second: float32 [4, 49152, 576], P('grp', 'wide'), may hold values from 1.5697491e-15 to 2.5115985e-14
- embed_table_anchor: float32 [49152, 576], P('wide')
- embed_table_momentum: float32 [49152, 576], P('wide'), may hold values from -0.3125 to 0.3125
- attn_in_master: float32 [4, 576, 960], P('grp', None, 'wide')
- attn_in_first: float32 [4, 576, 960], P('grp', None, 'wide'), may hold values from -2.861023e-06 to 2.861023e-06
- attn_in_second: float32 [4, 576, 960], P('grp', None, 'wide'), may hold values from 1.5697491e-15 to 2.5115985e-14
- attn_in_anchor: float32 [576, 960], P(None, 'wide')
- attn_in_momentum: float32 [576, 960], P(None, 'wide'), may hold values from -0.3125 to 0.3125
- ffn_in_master: float32 [4, 576, 3072], P('grp', None, 'wide')
- ffn_in_first: float32 [4, 576, 3072], P('grp', None, 'wide'), may hold values from -2.861023e-06 to 2.861023e-06
- ffn_in_second: float32 [4, 576, 3072], P('grp', None, 'wide'), may hold values from 1.5697491e-15 to 2.5115985e-14
- ffn_in_anchor: float32 [576, 3072], P(None, 'wide')
- ffn_in_momentum: float32 [576, 3072], P(None, 'wide'), may hold values from -0.3125 to 0.3125
- proj_out_master: float32 [4, 2112, 576], P('grp', None, 'wide')
- proj_out_first: float32 [4, 2112, 576], P('grp', None, 'wide'), may hold values from -2.861023e-06 to 2.861023e-06
- proj_out_second: float32 [4, 2112, 576], P('grp', None, 'wide'), may hold values from 1.5697491e-15 to 2.5115985e-14
- proj_out_anchor: float32 [2112, 576], P(None, 'wide')
- proj_out_momentum: float32 [2112, 576], P(None, 'wide'), may hold values from -0.3125 to 0.3125
- norm_gains_master: float32 [4, 3, 576], P('grp')
- norm_gains_first: float32 [4, 3, 576], P('grp'), may hold values from -3.0517578e-05 to 3.0517578e-05
- norm_gains_second: float32 [4, 3, 576], P('grp'), may hold values from 1.5697491e-13 to 2.5115986e-12
- norm_gains_anchor: float32 [3, 576], replicated
- norm_gains_momentum: float32 [3, 576], replicated, may hold values from -0.75 to 0.75
Outputs:
- loss_sum: float32 [4], P('grp')
- weight_total: float32 [4], P('grp')
- grad_norm: float32 [4], P('grp')
- embed_table_diff: float32 [49152, 576], P('wide')
- embed_table_outer: float32 [49152, 576], P('wide')
- embed_table_weight: float32 [49152, 576], P('wide')
- embed_table_first_new: float32 [4, 49152, 576], P('grp', 'wide')
- embed_table_second_new: float32 [4, 49152, 576], P('grp', 'wide')
- attn_in_diff: float32 [576, 960], P(None, 'wide')
- attn_in_outer: float32 [576, 960], P(None, 'wide')
- attn_in_weight: float32 [576, 960], P(None, 'wide')
- attn_in_first_new: float32 [4, 576, 960], P('grp', None, 'wide')
- attn_in_second_new: float32 [4, 576, 960], P('grp', None, 'wide')
- ffn_in_diff: float32 [576, 3072], P(None, 'wide')
- ffn_in_outer: float32 [576, 3072], P(None, 'wide')
- ffn_in_weight: float32 [576, 3072], P(None, 'wide')
- ffn_in_first_new: float32 [4, 576, 3072], P('grp', None, 'wide')
- ffn_in_second_new: float32 [4, 576, 3072], P('grp', None, 'wide')
- proj_out_diff: float32 [2112, 576], P(None, 'wide')
- proj_out_outer: float32 [2112, 576], P(None, 'wide')
- proj_out_weight: float32 [2112, 576], P(None, 'wide')
- proj_out_first_new: float32 [4, 2112, 576], P('grp', None, 'wide')
- proj_out_second_new: float32 [4, 2112, 576], P('grp', None, 'wide')
- norm_gains_diff: float32 [3, 576], replicated
- norm_gains_outer: float32 [3, 576], replicated
- norm_gains_weight: float32 [3, 576], replicated
- norm_gains_first_new: float32 [4, 3, 576], P('grp')
- norm_gains_second_new: float32 [4, 3, 576], P('grp')
Inputs may be any that keep to these rules, and one draw needn't show every extreme that they name: `row_counts`: each device's three counts sum to 1 (one row); along wide the source never falls within a group; each group's first device holds a web row and its last a math row.
All inputs are finite; a program needn't handle non-finite values.
Results may differ from a plain program's by a relative error of at most 0.019.
The roundings to bfloat16 on the way count: a program that leaves them out, or rounds other values in their place, can miss the bound.
Values may be sent and summed in bfloat16 or wider, within the bound.
A program may use at most 192 MiB of HBM per device.

v0:
```python
import functools

import jax
import jax.numpy as jnp
import numpy as np
from jax import lax
from jax.experimental import pallas as pl
from jax.experimental.pallas import tpu as pltpu
from jax.sharding import PartitionSpec as P

D = 576
H = 9
KVH = 3
HD = 64
FF = 1536
QKV = 960
STEP = 8
T = 256
SHARD = 1536
NW = 32
NG = 4
CAP = 32
FFN_AT, DOWN_AT, ATTN_AT, PACKED = 0, 96, 160, 208
SUMMED = 224

beta_one = 0.9
beta_two = 0.999
adam_eps = 1e-08
weight_decay = 0.1
inner_rate = 0.02
gain_rate = 0.2
clip_norm = 0.01
penalty_weight = 0.005
outer_rate = 0.7
outer_momentum = 0.9
rope_base = 100000.0
norm_eps = 1e-05
masked_score = -1e30

BF = jnp.bfloat16
F32 = jnp.float32
MESH = pl.DeviceIdType.MESH
VMEM = pl.BlockSpec(memory_space=pltpu.VMEM)
ANY = pl.BlockSpec(memory_space=pl.ANY)
DMA = pltpu.SemaphoreType.DMA
MIB = 1 << 20


def params(collective, mib):
    return pltpu.CompilerParams(
        collective_id=collective, has_side_effects=True, vmem_limit_bytes=mib * MIB
    )


def place():
    me = lax.axis_index("wide")
    return me, me // 8, lax.rem(me // 4, 2), lax.rem(me, 4)


def flat(y, xh, z):
    return y * 8 + xh * 4 + z


def turn4(at, by):
    return lax.rem(at + by, 4)


def remote(src, dst, ssem, rsem, **device):
    return pltpu.make_async_remote_copy(
        src_ref=src,
        dst_ref=dst,
        send_sem=ssem,
        recv_sem=rsem,
        device_id=device,
        device_id_type=MESH,
    )


def greet_wide(me, grp=None, sides=False, meanwhile=None):
    barrier = pltpu.get_barrier_semaphore()

    def one(k, carry):
        pl.semaphore_signal(
            barrier, inc=1, device_id={"wide": lax.rem(me + k, NW)}, device_id_type=MESH
        )
        return carry

    lax.fori_loop(1, NW, one, 0)
    count = NW - 1
    if grp is not None:
        for k in range(1, NG):
            pl.semaphore_signal(
                barrier, inc=1, device_id={"grp": lax.rem(grp + k, NG)}, device_id_type=MESH
            )
        count += NG - 1
    if sides:
        for step in (1, 3):
            pl.semaphore_signal(barrier, inc=1, device_id=beside(step), device_id_type=MESH)
        count += 2
    if meanwhile is not None:
        meanwhile()
    pl.semaphore_wait(barrier, count)


def near_peers(me, y, xh, z):
    peers = [flat(y, xh, turn4(z, k)) for k in (1, 2, 3)] + [flat(turn4(y, k), xh, z) for k in (1, 2, 3)]
    return peers + [flat(y, 1 - xh, z)]


class Tree:
    def __init__(self, hold, land_z, land_y, land_x, ssem, rsem):
        self.hold, self.lands = hold, (land_z, land_y, land_x)
        self.ssem, self.rsem = ssem, rsem
        me, self.y, self.xh, self.z = place()
        self.sent = []

    def send(self, stage):
        y, xh, z = self.y, self.xh, self.z
        at = (z, y, xh)[stage]
        land, src = self.lands[stage], self.hold.at[stage]
        for k in range(1, 2 if stage == 2 else 4):
            if stage == 0:
                to = flat(y, xh, turn4(z, k))
            elif stage == 1:
                to = flat(turn4(y, k), xh, z)
            else:
                to = flat(y, 1 - xh, z)
            copy = remote(src, land.at[at], self.ssem.at[stage, k], self.rsem.at[stage, at], wide=to)
            copy.start()
            self.sent.append(copy)
        land[at] = self.hold[stage]

    def start(self, value):
        self.hold[0] = value
        self.send(0)

    def collect(self, stage):
        at = (self.z, self.y, self.xh)[stage]
        land = self.lands[stage]
        size = 2 if stage == 2 else 4
        for k in range(1, size):
            other = lax.rem(at + k, size)
            remote(
                land.at[other], land.at[other], self.ssem.at[stage, k], self.rsem.at[stage, other],
                wide=flat(self.y, self.xh, self.z),
            ).wait_recv()
        total = land[0]
        for k in range(1, size):
            total = total + land[k]
        return total

    def next(self, stage):
        self.hold[stage + 1] = self.collect(stage)
        self.send(stage + 1)

    def finish(self):
        for copy in self.sent:
            copy.wait_send()


def tree_scratch(lanes):
    return [
        pltpu.VMEM((3, 8, lanes), F32),
        pltpu.VMEM((4, 8, lanes), F32),
        pltpu.VMEM((4, 8, lanes), F32),
        pltpu.VMEM((2, 8, lanes), F32),
        DMA((3, 4)),
        DMA((3, 4)),
    ]


class Scatter:
    def __init__(self, src_at, dst_at, ssem, rsem, me):
        self.src_at, self.dst_at, self.ssem, self.rsem, self.me = src_at, dst_at, ssem, rsem, me

    def copy(self, k):
        peer = lax.rem(self.me + k, NW)
        return remote(
            self.src_at(peer), self.dst_at(self.me), self.ssem.at[k], self.rsem.at[self.me], wide=peer
        )

    def start(self):
        def one(k, carry):
            self.copy(k).start()
            return carry

        lax.fori_loop(1, NW, one, 0)

    def wait_recv(self):
        def one(k, carry):
            peer = lax.rem(self.me + k, NW)
            remote(
                self.src_at(peer), self.dst_at(peer), self.ssem.at[k], self.rsem.at[peer], wide=peer
            ).wait_recv()
            return carry

        lax.fori_loop(1, NW, one, 0)

    def wait_send(self):
        def one(k, carry):
            self.copy(k).wait_send()
            return carry

        lax.fori_loop(1, NW, one, 0)


class Ring:
    def __init__(self, view, sem, bounds, ssem):
        self.view, self.sem, self.bounds = view, sem, bounds
        self.ssem, self.used, self.sent = ssem, 0, []
        self.me, self.y, self.xh, self.z = place()

    def send(self, src, dst, rsem, to):
        copy = remote(src, dst, self.ssem.at[self.used], rsem, wide=flat(to[0], self.xh, to[1]))
        self.used += 1
        copy.start()
        self.sent.append(copy)

    def piece(self, y, z, first, count):
        return self.view(y, z, self.bounds[first], self.bounds[first + count] - self.bounds[first])

    def pass_on(self, y, z, first, count, index, *to):
        piece = self.piece(y, z, first, count)
        for one in to:
            self.send(piece, piece, self.sem(y, z, index), one)

    def landed(self, piece, sem):
        remote(piece, piece, self.ssem.at[0], sem, wide=self.me).wait_recv()

    def wait(self, y, z, first, count, index):
        self.landed(self.piece(y, z, first, count), self.sem(y, z, index))

    def around(self):
        y, z = self.y, self.z
        return y, z, (turn4(y, 1), z), (turn4(y, 3), z), (y, turn4(z, 1)), (y, turn4(z, 3))

    def own(self, src, dst, index):
        y, z, y_up, y_down, z_up, z_down = self.around()
        for to in (y_up, y_down, z_up, z_down):
            self.send(src, dst, self.sem(y, z, index), to)

    def near(self, parts=None):
        y, z, y_up, y_down, z_up, z_down = self.around()
        for at, far, turn, half, sides in (
            (y_down, y_up, 0, 0, (z_up, z_down)),
            (y_up, y_down, 1, 0, (z_up, z_down)),
            (z_down, z_up, 0, 2, (y_up, y_down)),
            (z_up, z_down, 1, 2, (y_up, y_down)),
        ):
            if parts is None:
                self.wait(*at, 0, 4, 0)
            else:
                for part, index in parts:
                    self.landed(part(*at), self.sem(*at, index))
            self.pass_on(*at, turn, 1, turn, far)
            self.pass_on(*at, 2 + turn, 1, 2 + turn, far)
            self.pass_on(*at, half, 2, half, *sides)

    def far(self):
        y, z, y_up, y_down, z_up, z_down = self.around()
        for at, half, sides in (
            ((turn4(y, 2), z), 0, (z_up, z_down)),
            ((y, turn4(z, 2)), 2, (y_up, y_down)),
        ):
            for index in range(4):
                self.wait(*at, index, 1, index)
            self.pass_on(*at, half, 2, half, *sides)

    def cross(self):
        y, z, y_up, y_down, z_up, z_down = self.around()
        for k in (1, 3, 2):
            row, column = turn4(y, k), turn4(z, k)
            self.wait(row, z_down[1], 0, 2, 0)
            self.pass_on(row, z_down[1], 0, 1, 0, z_up)
            self.wait(row, z_up[1], 0, 2, 0)
            self.pass_on(row, z_up[1], 1, 1, 1, z_down)
            self.wait(y_down[0], column, 2, 2, 2)
            self.pass_on(y_down[0], column, 2, 1, 2, y_up)
            self.wait(y_up[0], column, 2, 2, 2)
            self.pass_on(y_up[0], column, 3, 1, 3, y_down)

    def last(self):
        y, z = self.y, self.z
        for k in (1, 3, 2):
            row, column = turn4(y, k), turn4(z, k)
            for index in range(2):
                self.wait(row, turn4(z, 2), index, 1, index)
                self.wait(turn4(y, 2), column, 2 + index, 1, 2 + index)

    def finish(self):
        for copy in self.sent:
            copy.wait_send()


RING_SENDS = 36


def beside(step):
    me, y, xh, z = place()
    grp = lax.axis_index("grp")
    low = grp // 2
    side = lax.rem(xh + low + (0 if step == 1 else 1), 2)
    return {"grp": (1 - low) * 2 + lax.rem(grp, 2), "wide": flat(y, side, z)}


class Relay:
    def __init__(self, sources, stops, ends, ssem, rsem):
        self.sources, self.stops, self.ends, self.ssem, self.rsem = sources, stops, ends, ssem, rsem

    def copy(self, src, dst, at, step):
        return remote(src, dst, self.ssem.at[at], self.rsem.at[at], **beside(step))

    def legs(self, hop):
        for i, step in enumerate((1, 3)):
            src = self.sources[i] if hop == 0 else self.stops[i]
            dst = self.stops[i] if hop == 0 else self.ends[i]
            yield self.copy(src, dst, 2 * hop + i, step)

    def start(self):
        for copy in self.legs(0):
            copy.start()

    def forward(self):
        for first, second in zip(self.legs(0), self.legs(1)):
            first.wait_recv()
            second.start()

    def wait(self):
        for copy in self.legs(1):
            copy.wait_recv()

    def finish(self):
        for hop in (0, 1):
            for copy in self.legs(hop):
                copy.wait_send()


def look_up(got, table, hot, rows, slot_row):
    asked = got[:, slot_row, :].astype(F32)
    asked = jnp.concatenate([asked, jnp.zeros((128 - NW, 128), F32)], 0).T
    step = 8 * CAP
    for first in range(0, NW, 8):
        for d in range(8):
            column = asked[0:CAP, first + d : first + d + 1]
            lanes = lax.broadcasted_iota(jnp.int32, (CAP, SHARD), 1).astype(F32)
            hot[d * CAP : (d + 1) * CAP, :] = jnp.where(lanes == column, 1.0, 0.0).astype(BF)
        picked = lax.dot_general(
            hot[...], table[...], (((1,), (1,)), ((), ())), preferred_element_type=F32
        )
        rows[first * CAP : first * CAP + step, :] = picked.astype(BF)


def slots(at):
    return pl.ds(pl.multiple_of(at * CAP, CAP), CAP)


def turn_over(table, rows, first):
    for c in range(0, SHARD, 256):
        rows[first + c : first + c + 256, :] = table[:, c : c + 256].T


def owner_of(ids):
    return (((ids >> 9) * 171) >> 9).astype(jnp.int32)


def ask_rows(tok, msg, picks, slot_out):
    row = tok[0:1, :]
    column = jnp.broadcast_to(row.astype(F32), (128, T)).T[:, 0:1].astype(jnp.int32)
    row_owner, column_owner = owner_of(row), owner_of(column)
    down = lax.broadcasted_iota(jnp.int32, (T, T), 0)
    across = lax.broadcasted_iota(jnp.int32, (T, T), 1)
    same = row == column

    def count(which, axis):
        return jnp.sum(jnp.where(which, 1.0, 0.0), axis, keepdims=True)

    first_row = count(same & (down < across), 0) == 0.0
    first_column = count(same & (across < down), 1) == 0.0
    near = row_owner == column_owner
    rank_row = count(near & (column < row) & first_column, 0)
    rank_column = count(near & (row < column) & first_row, 1)
    slot_row = jnp.where(rank_row < CAP, row_owner.astype(F32) * CAP + rank_row, -1.0)
    slot_column = jnp.where(rank_column < CAP, column_owner.astype(F32) * CAP + rank_column, -1.0)
    lanes = lax.broadcasted_iota(jnp.int32, (T, NW * CAP), 1).astype(F32)
    hit = lanes == slot_column
    picks[...] = jnp.where(hit, 1.0, 0.0).astype(BF)
    slot_out[...] = jnp.broadcast_to(slot_row, (8, T)).astype(jnp.int32)
    local = (column - column_owner * SHARD).astype(F32)
    asked = jnp.max(jnp.where(hit, local, -1.0), 0, keepdims=True).astype(jnp.int32)
    most = (jnp.max(rank_row, 1, keepdims=True) + 1.0).astype(jnp.int32)
    rest = [
        tok[1:2, 0:128], tok[1:2, 128:256], tok[3:4, 0:128], jnp.broadcast_to(most, (1, 128)),
    ] + [jnp.zeros((1, 128), jnp.int32)] * 3
    for g in range(8):
        msg[g] = jnp.concatenate([asked[:, g * 128 : (g + 1) * 128]] + rest, 0)


def find_rows(got, table, asked_t, hot, rows, part):
    asked = got[:, 0, :].astype(F32)
    asked_t[...] = jnp.concatenate([asked, jnp.full((128 - NW, 128), -1.0, F32)], 0).T
    mine = asked_t[pl.ds(pl.multiple_of(part * CAP, CAP), CAP), :]
    lanes = lax.broadcasted_iota(jnp.int32, (CAP, SHARD), 1).astype(F32)
    for d in range(NW):
        hot[d * CAP : (d + 1) * CAP, :] = jnp.where(lanes == mine[:, d : d + 1], 1.0, 0.0).astype(BF)
    step = 8 * CAP
    for first in range(0, NW * CAP, step):
        picked = lax.dot_general(
            hot[first : first + step, :], table[...], (((1,), (1,)), ((), ())), preferred_element_type=F32
        )
        rows[first : first + step, :] = picked.astype(BF)


def turn_over(table, rows, first):
    for c in range(0, SHARD, 256):
        rows[first + c : first + c + 256, :] = table[:, c : c + 256].T


def front_kernel(
    tok, table, packed, got, emb, most, table_other, rows_t, packed_all, picks, slot_out, hot, goal, weights,
    msg, asked_t, rows, own_most, stops, msg_s, msg_r, emb_s, emb_r, most_s, most_r, swap_s, swap_r,
    ring_s, ring_r, x_sem, local,
):
    me, y, xh, z = place()
    grp = lax.axis_index("grp")
    other = flat(y, 1 - xh, z)
    greet_wide(me, grp, sides=True, meanwhile=lambda: ask_rows(tok, msg, picks, slot_out))
    over = remote(packed, packed_all.at[y, z, xh], x_sem.at[0], x_sem.at[1], wide=other)
    over.start()
    ask = Scatter(lambda p: msg.at[p // 4], lambda p: got.at[p], msg_s, msg_r, me)
    ask.start()
    got[me] = msg[me // 4]
    ring = Ring(
        lambda Y, Z, first, count: packed_all.at[Y, Z, :, pl.ds(first, count)],
        lambda Y, Z, index: ring_r.at[Y, Z, index],
        (0, 48, 96, 144, 208),
        ring_s,
    )
    ring.own(packed, packed_all.at[y, z, xh], 0)
    keep = pltpu.make_async_copy(packed, packed_all.at[y, z, xh], local.at[0])
    keep.start()
    halves = (pl.ds(0, D // 2), pl.ds(D // 2, D // 2))
    trade = Relay(
        [table.at[half] for half in halves],
        [stops.at[i] for i in range(2)],
        [table_other.at[half] for half in halves],
        swap_s,
        swap_r,
    )
    trade.start()
    over.wait_recv()
    ring.own(packed_all.at[y, z, 1 - xh], packed_all.at[y, z, 1 - xh], 4)
    ask.wait_recv()
    find_rows(got, table, asked_t, hot, rows, lax.rem(me, 4))
    ring.near(
        [
            (lambda Y, Z: packed_all.at[Y, Z, xh], 0),
            (lambda Y, Z: packed_all.at[Y, Z, 1 - xh], 4),
        ]
    )
    reply = Scatter(lambda p: rows.at[slots(p)], lambda p: emb.at[slots(p)], emb_s, emb_r, me)
    reply.start()
    emb[slots(me), :] = rows[slots(me), :]
    turn_over(table, rows_t, 0)
    largest = jnp.max(got[:, 4, :], 0, keepdims=True)
    own_most[...] = jnp.broadcast_to(largest, (8, 128))
    most[grp] = own_most[...]
    told = []
    for k in range(1, NG):
        to = lax.rem(grp + k, NG)
        told.append(remote(own_most, most.at[grp], most_s.at[k], most_r.at[grp], grp=to))
        told[-1].start()
    total = jnp.sum(got[:, 3, :].astype(F32), 0, keepdims=True)
    total = jnp.concatenate([total, total], 1) * T
    plain = tok[3:4, :].astype(F32)
    weights[...] = jnp.concatenate([plain / total, plain, total] + [jnp.zeros((1, T), F32)] * 5, 0)

    def place_goal(j, carry):
        from_dev = flat(j // 4, xh, lax.rem(j, 4))
        goals = jnp.concatenate([got[from_dev, 1:2, :], got[from_dev, 2:3, :]], 1)
        near, far = goals - me * SHARD, goals - other * SHARD
        at = jnp.where((far >= 0) & (far < SHARD), far + SHARD, -1)
        at = jnp.where((near >= 0) & (near < SHARD), near, at)
        goal[j] = jnp.broadcast_to(at, (8, T))
        return carry

    lax.fori_loop(0, 16, place_goal, 0)
    ring.far()
    trade.forward()
    ring.cross()
    reply.wait_recv()
    for k in range(1, NG):
        to = lax.rem(grp + k, NG)
        remote(own_most, most.at[to], most_s.at[k], most_r.at[to], grp=to).wait_recv()
    trade.wait()
    turn_over(table_other, rows_t, SHARD)
    ring.last()
    keep.wait()
    over.wait_send()
    ask.wait_send()
    reply.wait_send()
    trade.finish()
    for copy in told:
        copy.wait_send()
    ring.finish()


def front(tok, table, packed):
    return pl.pallas_call(
        front_kernel,
        name="front",
        out_shape=(
            jax.ShapeDtypeStruct((NW, 8, 128), jnp.int32),
            jax.ShapeDtypeStruct((NW * CAP, D), BF),
            jax.ShapeDtypeStruct((NG, 8, 128), jnp.int32),
            jax.ShapeDtypeStruct((D, SHARD), BF),
            jax.ShapeDtypeStruct((2 * SHARD, D), BF),
            jax.ShapeDtypeStruct((4, 4, 2, PACKED, D), BF),
            jax.ShapeDtypeStruct((T, NW * CAP), BF),
            jax.ShapeDtypeStruct((8, T), jnp.int32),
            jax.ShapeDtypeStruct((NW * CAP, SHARD), BF),
            jax.ShapeDtypeStruct((16, 8, T), jnp.int32),
            jax.ShapeDtypeStruct((8, T), F32),
        ),
        in_specs=[VMEM, VMEM, ANY],
        out_specs=(VMEM, VMEM, VMEM, VMEM, VMEM, ANY) + (VMEM,) * 5,
        scratch_shapes=[
            pltpu.VMEM((8, 8, 128), jnp.int32),
            pltpu.VMEM((128, 128), F32),
            pltpu.VMEM((NW * CAP, D), BF),
            pltpu.VMEM((8, 128), jnp.int32),
            pltpu.VMEM((2, D // 2, SHARD), BF),
            DMA((NW,)),
            DMA((NW,)),
            DMA((NW,)),
            DMA((NW,)),
            DMA((NG,)),
            DMA((NG,)),
            DMA((4,)),
            DMA((4,)),
            DMA((RING_SENDS + 4,)),
            DMA((4, 4, 5)),
            DMA((2,)),
            DMA((1,)),
        ],
        compiler_params=params(1, 60),
        cost_estimate=pl.CostEstimate(flops=2 * 10**9, bytes_accessed=3 * 10**7, transcendentals=0),
    )(tok, table, packed)


ORDER = tuple((i // 8) * 8 + (i % 2) * 4 + (i // 2) % 4 for i in range(NW))


def spread_rows(used, stride, at, repeat=1):
    picks = np.zeros((NW * stride, NW * used), np.float32)
    for i, w in enumerate(ORDER):
        for j in range(repeat):
            for r in range(used):
                picks[i * stride + at + j * used + r, w * used + r] = 1.0
    return picks


def rope():
    half = HD // 2
    freqs = np.float32(rope_base) ** (-(np.arange(half, dtype=np.float32) * np.float32(2.0)) / np.float32(HD))
    angles = freqs.astype(np.float32)[:, None] * np.arange(T, dtype=np.float32)[None, :]
    return np.concatenate([np.cos(angles), np.sin(angles)], 0).astype(np.float32)


def turned(values):
    return values.T


def gain_columns(gains):
    return jnp.concatenate([gains[...], jnp.zeros((120, D), F32)], 0).T


def rms(values, gain):
    scale = lax.rsqrt(jnp.mean(values * values, 0, keepdims=True) + norm_eps)
    return values * scale * gain


def rms_back(values, gain, grad):
    scale = lax.rsqrt(jnp.mean(values * values, 0, keepdims=True) + norm_eps)
    pulled = grad * gain
    middle = jnp.mean(values * pulled, 0, keepdims=True)
    back = scale * pulled - values * (scale * scale * scale) * middle
    return back, jnp.sum(grad * values * scale, 1, keepdims=True)


def mask_of(tok):
    row = tok[2:3, :]
    column = jnp.broadcast_to(row.astype(F32), (128, T)).T[:, 0:1].astype(jnp.int32)
    down = lax.broadcasted_iota(jnp.int32, (T, T), 0)
    across = lax.broadcasted_iota(jnp.int32, (T, T), 1)
    return (down <= across) & (row == column)


def mm(a, b):
    return jnp.dot(a, b, preferred_element_type=F32)


def mm_nt(a, b):
    return lax.dot_general(a, b, (((1,), (1,)), ((), ())), preferred_element_type=F32)


def mm_tn(a, b):
    return lax.dot_general(a, b, (((0,), (0,)), ((), ())), preferred_element_type=F32)


def rotated(x, rot):
    cosine, sine = rot[0:32, :], rot[32:64, :]
    one, two = x[0:32, :], x[32:64, :]
    return jnp.concatenate([one * cosine - two * sine, two * cosine + one * sine], 0)


def unrotated(x, rot):
    cosine, sine = rot[0:32, :], rot[32:64, :]
    one, two = x[0:32, :], x[32:64, :]
    return jnp.concatenate([one * cosine + two * sine, two * cosine - one * sine], 0)


def load_trunk(packed, ffn, down, attn, sem):
    loads = [
        pltpu.make_async_copy(packed.at[:, :, :, ATTN_AT:PACKED], attn, sem.at[0]),
        pltpu.make_async_copy(packed.at[:, :, :, FFN_AT:DOWN_AT], ffn, sem.at[1]),
        pltpu.make_async_copy(packed.at[:, :, :, DOWN_AT:ATTN_AT, 0:512], down, sem.at[2]),
    ]
    for load in loads:
        load.start()
    return loads


TRUNK_SCRATCH = [
    pltpu.VMEM((4, 4, 2, 96, D), BF),
    pltpu.VMEM((4, 4, 2, 64, 512), BF),
    pltpu.VMEM((4, 4, 2, 48, D), BF),
    DMA((3,)),
]


def forward_kernel(
    more, emb, picks, packed, gains, rot, tok,
    final, h0, n1, q, k, v, lse, att, h1, n2, gate_up, inner, h2,
    ffn, down, attn, sem, mixed,
):
    loads = load_trunk(packed, ffn, down, attn, sem)
    columns = gain_columns(gains)
    allowed = mask_of(tok)
    start = turned(mm(picks[...], emb[...]) + more[...])
    h0[...] = start
    normed = rms(start, columns[:, 0:1]).astype(BF)
    n1[...] = normed
    loads[0].wait()
    rows48 = attn[...].reshape(NW * 48, D)
    product = mm(rows48, normed)
    for i, w in enumerate(ORDER):
        mixed[w * 30 : w * 30 + 30, :] = product[i * 48 : i * 48 + 30, :]
    for kv in range(KVH):
        k[kv * HD : (kv + 1) * HD, :] = rotated(
            mixed[D + kv * HD : D + (kv + 1) * HD, :], rot[...]
        ).astype(BF)
        at = D + (KVH + kv) * HD
        v[kv * HD : (kv + 1) * HD, :] = mixed[at : at + HD, :].astype(BF)
    logs = []
    for h in range(H):
        kv = h // (H // KVH)
        query = rotated(mixed[h * HD : (h + 1) * HD, :], rot[...]).astype(BF)
        q[h * HD : (h + 1) * HD, :] = query
        scores = mm_tn(k[kv * HD : (kv + 1) * HD, :], query) * HD ** (-0.5)
        scores = jnp.where(allowed, scores, masked_score)
        top = jnp.max(scores, 0, keepdims=True)
        power = jnp.exp(scores - top)
        total = jnp.sum(power, 0, keepdims=True)
        probs = (power / total).astype(BF)
        att[h * HD : (h + 1) * HD, :] = mm(v[kv * HD : (kv + 1) * HD, :], probs).astype(BF)
        logs.append(top + jnp.log(total))
    lse[...] = jnp.concatenate(logs + [jnp.zeros((16 - H, T), F32)], 0)
    product = mm(rows48, att[...])
    for i, w in enumerate(ORDER):
        mixed[w * 18 : w * 18 + 18, :] = product[i * 48 + 30 : i * 48 + 48, :]
    middle = start + mixed[0:D, :]
    h1[...] = middle
    normed = rms(middle, columns[:, 1:2]).astype(BF)
    n2[...] = normed
    loads[1].wait()
    gate_up[...] = mm(ffn[...].reshape(NW * 96, D), normed)
    for i in range(NW // 2):
        gate = gate_up[i * 96 : (i + 1) * 96, :]
        up = gate_up[FF + i * 96 : FF + (i + 1) * 96, :]
        w = ORDER[i]
        inner[w * 96 : (w + 1) * 96, :] = (gate / (1.0 + jnp.exp(-gate)) * up).astype(BF)
    loads[2].wait()
    rows64 = down[...].reshape(NW * 64, 512)
    for j in range(3):
        product = mm(rows64, inner[j * 512 : (j + 1) * 512, :])
        for i, w in enumerate(ORDER):
            piece = product[i * 64 + j * 18 : i * 64 + j * 18 + 18, :]
            if j:
                mixed[w * 18 : w * 18 + 18, :] += piece
            else:
                mixed[w * 18 : w * 18 + 18, :] = piece
    last = middle + mixed[0:D, :]
    h2[...] = last
    final[...] = rms(last, columns[:, 2:3]).astype(BF)


def forward(more, emb, picks, packed, gains, rot, tok):
    def out(rows, kind):
        return jax.ShapeDtypeStruct((rows, T), kind)

    return pl.pallas_call(
        forward_kernel,
        name="forward",
        out_shape=(
            out(D, BF), out(D, F32), out(D, BF), out(D, BF), out(KVH * HD, BF), out(KVH * HD, BF), out(16, F32),
            out(D, BF), out(D, F32), out(D, BF), out(2 * FF, F32), out(FF, BF), out(D, F32),
        ),
        in_specs=[VMEM, VMEM, VMEM, ANY, VMEM, VMEM, VMEM],
        out_specs=(VMEM,) * 13,
        scratch_shapes=TRUNK_SCRATCH + [pltpu.VMEM((QKV, T), F32)],
        compiler_params=pltpu.CompilerParams(vmem_limit_bytes=60 * MIB),
        cost_estimate=pl.CostEstimate(flops=4 * 10**9, bytes_accessed=2 * 10**7, transcendentals=10**6),
    )(more, emb, picks, packed, gains, rot, tok)


def more_rows_kernel(msg, table, got, emb, hot, rows, msg_s, msg_r, emb_s, emb_r):
    me = lax.axis_index("wide")
    greet_wide(me)
    ask = Scatter(lambda p: msg.at[p], lambda p: got.at[p], msg_s, msg_r, me)
    ask.start()
    got[me] = msg[me]
    ask.wait_recv()
    look_up(got, table, hot, rows, 0)
    reply = Scatter(lambda p: rows.at[slots(p)], lambda p: emb.at[slots(p)], emb_s, emb_r, me)
    reply.start()
    emb[slots(me), :] = rows[slots(me), :]
    reply.wait_recv()
    ask.wait_send()
    reply.wait_send()


def more_rows(msg, table):
    return pl.pallas_call(
        more_rows_kernel,
        name="more_rows",
        out_shape=(
            jax.ShapeDtypeStruct((NW, 8, 128), jnp.int32),
            jax.ShapeDtypeStruct((NW * CAP, D), BF),
        ),
        in_specs=[VMEM, VMEM],
        out_specs=(VMEM, VMEM),
        scratch_shapes=[pltpu.VMEM((8 * CAP, SHARD), BF), pltpu.VMEM((NW * CAP, D), BF)]
        + [DMA((NW,))] * 4,
        compiler_params=params(2, 40),
    )(msg, table)[1]


def more_grads_kernel(msg, rows, got, out, msg_s, msg_r, row_s, row_r):
    me = lax.axis_index("wide")
    greet_wide(me)
    ask = Scatter(lambda p: msg.at[p], lambda p: got.at[p], msg_s, msg_r, me)
    ask.start()
    give = Scatter(lambda p: rows.at[slots(p)], lambda p: out.at[slots(p)], row_s, row_r, me)
    give.start()
    got[me] = msg[me]
    out[slots(me), :] = rows[slots(me), :]
    ask.wait_recv()
    give.wait_recv()
    ask.wait_send()
    give.wait_send()


def more_grads(msg, rows):
    return pl.pallas_call(
        more_grads_kernel,
        name="more_grads",
        out_shape=(
            jax.ShapeDtypeStruct((NW, 8, 128), jnp.int32),
            jax.ShapeDtypeStruct((NW * CAP, D), BF),
        ),
        in_specs=[VMEM, VMEM],
        out_specs=(VMEM, VMEM),
        scratch_shapes=[DMA((NW,))] * 4,
        compiler_params=params(3, 20),
    )(msg, rows)


VOC = 2 * SHARD
TOK = 16 * T
CH = 512
NCH = VOC // CH
QUART = D // 4


def cols(j):
    return pl.ds(pl.multiple_of(j * T, T), T)


def head_kernel(
    final, rows_t, table, table_other, goal, weights,
    grad_final, head_own, head_other, loss,
    fall, expo, even, odd_grad, tops, stat, stat_in, coef, coef_in, parts,
    part_a, part_b, whole_a, whole_b, sum_a, sum_b, part_a2, part_b2, whole_a2, whole_b2,
    g_s, g_r, st_s, st_r, co_s, co_r, a_s, b_s, pa_r, pb_r, wa_r, wb_r, a2_s, b2_s, a2_r, b2_r,
):
    me, y, xh, z = place()
    mine = y * 4 + z

    def dev(j):
        return flat(j // 4, xh, lax.rem(j, 4))

    barrier = pltpu.get_barrier_semaphore()

    def greet(k, carry):
        pl.semaphore_signal(
            barrier, inc=1, device_id={"wide": dev(lax.rem(mine + k, 16))}, device_id_type=MESH
        )
        return carry

    lax.fori_loop(1, 16, greet, 0)
    pl.semaphore_wait(barrier, 15)

    sent = []

    def send(src, dst, ssem, rsem, to):
        copy = remote(src, dst, ssem, rsem, wide=to)
        copy.start()
        sent.append(copy)

    def arrived(dst, rsem):
        remote(dst, dst, g_s.at[0], rsem, wide=dev(mine)).wait_recv()

    ring = Ring(
        lambda Y, Z, first, count: fall.at[pl.ds(first, count), cols(Y * 4 + Z)],
        lambda Y, Z, index: g_r.at[Y * 4 + Z, index],
        tuple(QUART * k for k in range(5)),
        g_s,
    )
    ring.own(final, fall.at[:, cols(mine)], 0)
    fall[:, cols(mine)] = final[...]

    def logits(j):
        seen = fall[:, cols(j)]
        goals = goal[j]
        group, hit = goals >> 3, jnp.zeros((8, T), F32)
        tip, weight = [], []
        ahead = mm(rows_t[0:CH, :], seen)
        for c in range(NCH):
            part = ahead
            if c + 1 < NCH:
                ahead = mm(rows_t[(c + 1) * CH : (c + 2) * CH, :], seen)
            top = jnp.max(part, 0, keepdims=True)
            power = jnp.exp(part - top)
            for r in range(CH // 8):
                hit = jnp.where(group == c * (CH // 8) + r, part[8 * r : 8 * r + 8, :], hit)
            expo[c * CH : (c + 1) * CH, cols(j)] = power.astype(BF)
            tip.append(top)
            weight.append(jnp.sum(power, 0, keepdims=True))
        spot = lax.broadcasted_iota(jnp.int32, (8, T), 0)
        hit = jnp.sum(jnp.where(spot == (goals & 7), hit, 0.0), 0, keepdims=True)
        top = functools.reduce(jnp.maximum, tip)
        total = sum(w * jnp.exp(t - top) for w, t in zip(weight, tip))
        zero = jnp.zeros((1, T), F32)
        tops[j] = jnp.concatenate(tip + [zero] * (8 - NCH), 0)
        stat[j] = jnp.concatenate([top, total, hit] + [zero] * 5, 0)

    def tell(j):
        return remote(stat.at[j], stat_in.at[mine], st_s.at[j], st_r.at[mine], wide=dev(j))

    def block(dy, dz):
        return turn4(y, dy) * 4 + turn4(z, dz)

    def forward(offsets):
        def one(k, carry):
            j = block(*offsets(k))
            logits(j)
            tell(j).start()
            return carry

        return one

    def odd(k):
        return 1 + 2 * lax.rem(k, 2)

    logits(mine)
    stat_in[mine] = stat[mine]
    ring.near()
    lax.fori_loop(0, 4, forward(lambda k: ((1 - k // 2) * odd(k), (k // 2) * odd(k))), 0)
    ring.far()
    lax.fori_loop(0, 2, forward(lambda k: (2 * (1 - k), 2 * k)), 0)
    ring.cross()
    lax.fori_loop(0, 4, forward(lambda k: (odd(k // 2), odd(k))), 0)
    ring.last()
    lax.fori_loop(
        0,
        4,
        forward(lambda k: (2 * (1 - k // 2) + odd(k) * (k // 2), odd(k) * (1 - k // 2) + 2 * (k // 2))),
        0,
    )
    forward(lambda k: (2, 2))(0, 0)

    def hear(k, carry):
        j = lax.rem(mine + k, 16)
        arrived(stat_in.at[j], st_r.at[j])
        return carry

    lax.fori_loop(1, 16, hear, 0)
    tip, weight, hit = stat_in[:, 0, :], stat_in[:, 1, :], stat_in[:, 2, :]
    top = jnp.max(tip, 0, keepdims=True)
    lse = top + jnp.log(jnp.sum(weight * jnp.exp(tip - top), 0, keepdims=True))
    picked = jnp.sum(hit, 0, keepdims=True)
    share, plain = weights[0:1, :], weights[1:2, :]
    zero = jnp.zeros((1, T), F32)
    coef[...] = jnp.concatenate(
        [lse, share * (1.0 + 2.0 * penalty_weight * lse), share] + [zero] * 5, 0
    )
    loss[...] = jnp.concatenate(
        [plain * (lse - picked + penalty_weight * lse * lse)] + [zero] * 7, 0
    )
    coef_in[mine] = coef[...]

    def spread(k):
        j = lax.rem(mine + k, 16)
        return remote(coef, coef_in.at[mine], co_s.at[k], co_r.at[mine], wide=dev(j))

    def spread_start(k, carry):
        spread(k).start()
        return carry

    lax.fori_loop(1, 16, spread_start, 0)

    up, down = 1, 3
    z_to = {step: flat(y, xh, turn4(z, step)) for step in (up, down)}
    y_to = {step: flat(turn4(y, step), xh, z) for step in (up, down)}

    def piece_a(j, index):
        row = j // 4
        return remote(
            parts.at[j, pl.ds(index * QUART, QUART)], part_a.at[index, row],
            a_s.at[j, index], pa_r.at[index, row], wide=z_to[(up, down)[index]],
        )

    def piece_b(j, index):
        column = lax.rem(j, 4)
        return remote(
            parts.at[j, pl.ds((2 + index) * QUART, QUART)], part_b.at[index, column],
            b_s.at[j, index], pb_r.at[index, column], wide=y_to[(up, down)[index]],
        )

    def half_a(j, index):
        row = j // 4
        return remote(
            parts.at[j, pl.ds(0, 2 * QUART)], whole_a.at[index, row],
            a_s.at[j, 0], wa_r.at[index, row], wide=z_to[(up, down)[index]],
        )

    def half_b(j, index):
        column = lax.rem(j, 4)
        return remote(
            parts.at[j, pl.ds(2 * QUART, 2 * QUART)], whole_b.at[index, column],
            b_s.at[j, 0], wb_r.at[index, column], wide=y_to[(up, down)[index]],
        )

    def offsets(k):
        return lax.rem(2 + k // 4, 4), lax.rem(2 + k, 4)

    def post(k):
        dy, dz = offsets(k)
        j = block(dy, dz)

        @pl.when(dz == 2)
        def _():
            piece_a(j, 0).start()
            piece_a(j, 1).start()

        @pl.when(dy == 2)
        def _():
            piece_b(j, 0).start()
            piece_b(j, 1).start()

        for index, step in enumerate((up, down)):

            @pl.when(dz == step)
            def _():
                row = j // 4
                arrived(part_a.at[index, row], pa_r.at[index, row])
                rows = pl.ds(index * QUART, QUART)
                total = parts[j, rows, :].astype(F32) + part_a[index, row].astype(F32)
                parts[j, rows, :] = total.astype(BF)
                half_a(j, index).start()

            @pl.when(dy == step)
            def _():
                column = lax.rem(j, 4)
                arrived(part_b.at[index, column], pb_r.at[index, column])
                rows = pl.ds((2 + index) * QUART, QUART)
                total = parts[j, rows, :].astype(F32) + part_b[index, column].astype(F32)
                parts[j, rows, :] = total.astype(BF)
                half_b(j, index).start()

    def await_coef(k):
        j = block(*offsets(k))

        @pl.when(k != 10)
        def _():
            arrived(coef_in.at[j], co_r.at[j])

    def grad_logits(k, out):
        j = block(*offsets(k))
        lse, soft, pick = coef_in[j, 0:1, :], coef_in[j, 1:2, :], coef_in[j, 2:3, :]
        goals = goal[j]
        group = goals >> 3
        pick = jnp.where(lax.broadcasted_iota(jnp.int32, (8, T), 0) == (goals & 7), pick, 0.0)
        for c in range(NCH):
            scale = soft * jnp.exp(tops[j, c : c + 1, :] - lse)
            power = expo[c * CH : (c + 1) * CH, cols(j)].astype(F32)
            spot = lax.broadcasted_iota(jnp.int32, (CH // 8, 8, T), 0) + c * (CH // 8)
            drop = jnp.where(spot == group[None], pick[None], 0.0).reshape(CH, T)
            grad = (power * scale - drop).astype(BF)
            out[c * CH : (c + 1) * CH, :] = grad
            expo[c * CH : (c + 1) * CH, cols(j)] = grad

    def to_tokens(k, grad):
        product = mm(table[...], grad[0:SHARD, :]) + mm(table_other[...], grad[SHARD:VOC, :])
        parts[block(*offsets(k))] = product.astype(BF)

    def backward(i, carry):
        for k, now, ahead in ((2 * i, even, odd_grad), (2 * i + 1, odd_grad, even)):
            await_coef(k + 1)
            to_tokens(k, now)
            grad_logits(k + 1, ahead)

            @pl.when(k > 0)
            def _():
                post(k - 1)

        return carry

    await_coef(0)
    grad_logits(0, even)
    lax.fori_loop(0, 7, backward, 0)
    await_coef(15)
    to_tokens(14, even)
    grad_logits(15, odd_grad)
    post(13)
    to_tokens(15, odd_grad)
    post(14)
    post(15)

    def head_chunk(c):
        return lax.dot_general(
            fall[...],
            expo[pl.ds(pl.multiple_of(c * 256, 256), 256), :],
            (((1,), (1,)), ((), ())),
            preferred_element_type=F32,
        )

    def other_chunk(c, carry):
        head_other[:, cols(c)] = head_chunk(c + SHARD // 256).astype(BF)
        return carry

    def own_chunk(c, carry):
        head_own[:, cols(c)] = head_chunk(c)
        return carry

    lax.fori_loop(0, SHARD // 256, other_chunk, 0)

    kinds = (
        (whole_a, wa_r, sum_a, part_a2, whole_a2, a2_s, a2_r, y_to, 0),
        (whole_b, wb_r, sum_b, part_b2, whole_b2, b2_s, b2_r, z_to, 2 * QUART),
    )
    for d in (2, 1, 3, 0):
        for kind, (whole, w_r, total, part2, whole2, s2, r2, to, base) in enumerate(kinds):
            at = turn4(y if kind == 0 else z, d)
            j = at * 4 + z if kind == 0 else y * 4 + at
            acc = parts[j, base : base + 2 * QUART, :].astype(F32)
            for index in range(2):
                arrived(whole.at[index, at], w_r.at[index, at])
                acc = acc + whole[index, at].astype(F32)
            if d == 0:
                grad_final[base : base + 2 * QUART, :] = acc
            else:
                total[d - 1] = acc.astype(BF)
            if d == 2:
                for index, step in enumerate((up, down)):
                    piece = total.at[1, pl.ds(index * QUART, QUART)]
                    send(piece, part2.at[index], s2.at[index], r2.at[index], to[step])
    lax.fori_loop(0, SHARD // 512, own_chunk, 0)
    for kind, (whole, w_r, total, part2, whole2, s2, r2, to, base) in enumerate(kinds):
        for index, step in enumerate((up, down)):
            arrived(part2.at[index], r2.at[index])
            rows = pl.ds(index * QUART, QUART)
            added = total[step - 1, rows, :].astype(F32) + part2[index].astype(F32)
            total[step - 1, rows, :] = added.astype(BF)
            send(total.at[step - 1], whole2.at[index], s2.at[2 + index], r2.at[2 + index], to[step])
    lax.fori_loop(SHARD // 512, SHARD // 256, own_chunk, 0)
    for kind, (whole, w_r, total, part2, whole2, s2, r2, to, base) in enumerate(kinds):
        for index in range(2):
            arrived(whole2.at[index], r2.at[2 + index])
        grad_final[base : base + 2 * QUART, :] += whole2[0].astype(F32) + whole2[1].astype(F32)

    def finish(k, carry):
        j = lax.rem(mine + k, 16)
        tell(j).wait_send()
        spread(k).wait_send()
        return carry

    lax.fori_loop(1, 16, finish, 0)
    for copy in sent:
        copy.wait_send()
    ring.finish()

    def finish_pieces(k, carry):
        row, column = block(k, 2), block(2, k)
        piece_a(row, 0).wait_send()
        piece_a(row, 1).wait_send()
        piece_b(column, 0).wait_send()
        piece_b(column, 1).wait_send()
        for index, step in enumerate((up, down)):
            half_a(block(k, step), index).wait_send()
            half_b(block(step, k), index).wait_send()
        return carry

    lax.fori_loop(0, 4, finish_pieces, 0)


def head(final, rows_t, table, table_other, goal, weights):
    return pl.pallas_call(
        head_kernel,
        name="head",
        out_shape=(
            jax.ShapeDtypeStruct((D, T), F32),
            jax.ShapeDtypeStruct((D, SHARD), F32),
            jax.ShapeDtypeStruct((D, SHARD), BF),
            jax.ShapeDtypeStruct((8, T), F32),
        ),
        in_specs=[VMEM] * 6,
        out_specs=(VMEM,) * 4,
        scratch_shapes=[
            pltpu.VMEM((D, TOK), BF),
            pltpu.VMEM((VOC, TOK), BF),
            pltpu.VMEM((VOC, T), BF),
            pltpu.VMEM((VOC, T), BF),
            pltpu.VMEM((16, 8, T), F32),
            pltpu.VMEM((16, 8, T), F32),
            pltpu.VMEM((16, 8, T), F32),
            pltpu.VMEM((8, T), F32),
            pltpu.VMEM((16, 8, T), F32),
            pltpu.VMEM((16, D, T), BF),
            pltpu.VMEM((2, 4, QUART, T), BF),
            pltpu.VMEM((2, 4, QUART, T), BF),
            pltpu.VMEM((2, 4, 2 * QUART, T), BF),
            pltpu.VMEM((2, 4, 2 * QUART, T), BF),
            pltpu.VMEM((3, 2 * QUART, T), BF),
            pltpu.VMEM((3, 2 * QUART, T), BF),
            pltpu.VMEM((2, QUART, T), BF),
            pltpu.VMEM((2, QUART, T), BF),
            pltpu.VMEM((2, 2 * QUART, T), BF),
            pltpu.VMEM((2, 2 * QUART, T), BF),
            DMA((RING_SENDS,)),
            DMA((16, 4)),
            DMA((16,)),
            DMA((16,)),
            DMA((16,)),
            DMA((16,)),
            DMA((16, 2)),
            DMA((16, 2)),
            DMA((2, 4)),
            DMA((2, 4)),
            DMA((2, 4)),
            DMA((2, 4)),
            DMA((4,)),
            DMA((4,)),
            DMA((4,)),
            DMA((4,)),
        ],
        compiler_params=params(4, 61),
        cost_estimate=pl.CostEstimate(
            flops=6 * VOC * TOK * D, bytes_accessed=2 * 10**7, transcendentals=VOC * TOK
        ),
    )(final, rows_t, table, table_other, goal, weights)


class Reduce:
    def __init__(self, parts, base, sizes, along_z, refs):
        (
            self.first, part_a, part_b, self.whole1, self.second, next_a, next_b, self.whole2,
            self.third, self.stop, self.third_in, self.s, self.r,
        ) = refs
        self.part1, self.part2 = (part_a, part_b), (next_a, next_b)
        self.parts, self.base, self.sizes, self.along_z = parts, base, sizes, along_z
        self.rows = (pl.ds(0, sizes[0]), pl.ds(sizes[0], sizes[1]), pl.ds(0, sum(sizes)))
        self.me, self.y, self.xh, self.z = place()
        self.sent = []

    def send(self, src, dst, at, **to):
        copy = remote(src, dst, self.s.at[at], self.r.at[at], **to)
        copy.start()
        self.sent.append(copy)

    def wait(self, dst, at):
        remote(dst, dst, self.s.at[at], self.r.at[at], wide=self.me).wait_recv()

    def item1(self, step, which):
        rows = pl.ds(self.base + self.rows[which].start, self.rows[which].size)
        if self.along_z:
            return (slice(None), turn4(self.z, step), slice(None), rows)
        return (turn4(self.y, step), slice(None), slice(None), rows)

    def item2(self, step, which):
        return (turn4(self.y if self.along_z else self.z, step), slice(None), self.rows[which])

    def to(self, stage, step):
        if self.along_z == (stage == 1):
            return flat(self.y, self.xh, turn4(self.z, step))
        return flat(turn4(self.y, step), self.xh, self.z)

    def split(self, stage, ref, item, part, base):
        for index, step in enumerate((1, 3)):
            self.send(ref.at[item(2, index)], part[index], base + index, wide=self.to(stage, step))

    def join(self, stage, ref, item, part, whole, base):
        for index, step in enumerate((1, 3)):
            self.wait(part[index], base + index)
            at = item(step, index)
            ref[at] = (ref[at].astype(F32) + part[index][...].astype(F32)).astype(BF)
            self.send(ref.at[item(step, 2)], whole.at[index], base + 2 + index, wide=self.to(stage, step))

    def add(self, ref, item, whole, base):
        acc = ref[item(0, 2)].astype(F32)
        for index in range(2):
            self.wait(whole.at[index], base + 2 + index)
            acc = acc + whole[index].astype(F32)
        return acc

    def one(self):
        self.split(1, self.parts, self.item1, self.part1, 0)

    def two(self):
        self.join(1, self.parts, self.item1, self.part1, self.whole1, 0)

    def three(self):
        self.first[...] = self.add(self.parts, self.item1, self.whole1, 0).astype(BF)
        self.split(2, self.first, self.item2, self.part2, 4)

    def four(self):
        self.join(2, self.first, self.item2, self.part2, self.whole2, 4)

    def five(self):
        self.second[...] = self.add(self.first, self.item2, self.whole2, 4)
        self.third[...] = self.second[1 - self.xh].astype(BF)
        self.send(self.third, self.stop, 8, **beside(1 if self.along_z else 3))

    def six(self):
        self.wait(self.stop, 8)
        self.send(self.stop, self.third_in, 9, **beside(1 if self.along_z else 3))

    def total(self):
        self.wait(self.third_in, 9)
        return self.second[self.xh] + self.third_in[...].astype(F32)

    def finish(self):
        for copy in self.sent:
            copy.wait_send()


STREAMS = ((0, (48, 32), True), (80, (48, 32), False), (160, (16, 16), True), (192, (16, 16), False))


def reduce_scratch():
    shapes = []
    for _, sizes, _ in STREAMS:
        half = sum(sizes)
        shapes += [
            pltpu.VMEM((4, 2, half, D), BF),
            pltpu.VMEM((4, 2, sizes[0], D), BF),
            pltpu.VMEM((4, 2, sizes[1], D), BF),
            pltpu.VMEM((2, 4, 2, half, D), BF),
            pltpu.VMEM((2, half, D), F32),
            pltpu.VMEM((2, sizes[0], D), BF),
            pltpu.VMEM((2, sizes[1], D), BF),
            pltpu.VMEM((2, 2, half, D), BF),
            pltpu.VMEM((half, D), BF),
            pltpu.VMEM((half, D), BF),
            pltpu.VMEM((half, D), BF),
            DMA((10,)),
            DMA((10,)),
        ]
    return shapes


def back_kernel(
    grad_final, h0, n1, q, k, v, lse, att, h1, n2, gate_up, inner, h2,
    packed, gains, rot, tok, slot_row, loss, head_other, lay_attn_in, lay_out_in, lay_down_in,
    summed, rows_in, head_in, extra_sum, grad_embedded,
    ffn, down, attn, sem, lay_attn, lay_out, lay_down, lay_sem, parts, rows, grad_up, grad_mixed, spread, stops,
    row_s, row_r, swap_s, swap_r, hold, land_z, land_y, land_x, tree_s, tree_r, *reducers,
):
    me, y, xh, z = place()
    lays = [
        pltpu.make_async_copy(src, dst, lay_sem.at[i])
        for i, (src, dst) in enumerate(
            ((lay_down_in, lay_down), (lay_out_in, lay_out), (lay_attn_in, lay_attn))
        )
    ]
    lays[0].start()
    loads = load_trunk(packed, ffn, down, attn, sem)
    lays[1].start()
    lays[2].start()
    greet_wide(me, sides=True)
    halves = (pl.ds(0, D // 2), pl.ds(D // 2, D // 2))
    trade = Relay(
        [head_other.at[half] for half in halves],
        [stops.at[i] for i in range(2)],
        [head_in.at[half] for half in halves],
        swap_s,
        swap_r,
    )
    trade.start()
    streams = [
        Reduce(parts, base, sizes, along, reducers[13 * i : 13 * i + 13])
        for i, (base, sizes, along) in enumerate(STREAMS)
    ]
    early, late = streams[:2], streams[2:]
    columns = gain_columns(gains)

    grad_h2, gain3 = rms_back(h2[...], columns[:, 2:3], grad_final[...])
    lays[0].wait()
    spread[...] = mm(lay_down[...], grad_h2.astype(BF)).astype(BF)
    chunk = lax.broadcasted_iota(jnp.int32, (NW * 64, T), 0) & 63
    zero = jnp.zeros((NW * 64, T), BF)
    wide = jnp.concatenate(
        [
            jnp.where((chunk >= 18 * j) & (chunk < 18 * (j + 1)), spread[...].astype(F32), 0.0).astype(BF)
            for j in range(3)
        ],
        1,
    )
    inners = jnp.concatenate([inner[j * 512 : (j + 1) * 512, :] for j in range(3)], 1)
    grad_down = mm_nt(wide, inners).astype(BF).reshape(4, 4, 2, 64, 512)
    parts[:, :, :, DOWN_AT:ATTN_AT, 0:512] = grad_down
    parts[:, :, :, DOWN_AT:ATTN_AT, 512:D] = jnp.zeros((4, 4, 2, 64, D - 512), BF)
    loads[2].wait()
    grad_inner = mm_tn(down[...].reshape(NW * 64, 512), wide)
    for i in range(NW // 2):
        w = ORDER[i]
        gate = gate_up[i * 96 : (i + 1) * 96, :]
        up = gate_up[FF + i * 96 : FF + (i + 1) * 96, :]
        pieces = []
        for at in range(w * 96, w * 96 + 96, 32):
            j, r = at // 512, at % 512
            pieces.append(grad_inner[r : r + 32, j * T : (j + 1) * T])
        grad = jnp.concatenate(pieces, 0)
        sigmoid = 1.0 / (1.0 + jnp.exp(-gate))
        slope = sigmoid * (1.0 + gate * (1.0 - sigmoid))
        grad_up[i * 96 : (i + 1) * 96, :] = (grad * up * slope).astype(BF)
        grad_up[FF + i * 96 : FF + (i + 1) * 96, :] = (grad * (gate * sigmoid)).astype(BF)
    parts[:, :, :, FFN_AT:DOWN_AT, :] = mm_nt(grad_up[...], n2[...]).astype(BF).reshape(4, 4, 2, 96, D)
    for stream in early:
        stream.one()
    loads[1].wait()
    grad_normed = turned(mm_tn(grad_up[...], ffn[...].reshape(NW * 96, D)))
    part, gain2 = rms_back(h1[...], columns[:, 1:2], grad_normed)
    grad_h1 = grad_h2 + part
    lays[1].wait()
    out_rows = mm(lay_out[...], grad_h1.astype(BF)).astype(BF)
    loads[0].wait()
    rows48 = attn[...].reshape(NW * 48, D)
    grad_att = turned(mm_tn(out_rows, rows48)).astype(BF)
    for stream in early:
        stream.two()

    allowed = mask_of(tok)
    group = H // KVH
    for kv in range(KVH):
        keys = k[kv * HD : (kv + 1) * HD, :]
        values = v[kv * HD : (kv + 1) * HD, :]
        grad_k, grad_v = jnp.zeros((HD, T), F32), jnp.zeros((HD, T), F32)
        for h in range(kv * group, (kv + 1) * group):
            query = q[h * HD : (h + 1) * HD, :]
            grad_out = grad_att[h * HD : (h + 1) * HD, :]
            scores = mm_tn(keys, query) * HD ** (-0.5)
            scores = jnp.where(allowed, scores, masked_score)
            soft = jnp.exp(scores - lse[h : h + 1, :])
            grad_probs = mm_tn(values, grad_out)
            mean = jnp.sum(soft * grad_probs, 0, keepdims=True)
            grad_scores = (soft * (grad_probs - mean)).astype(BF)
            grad_q = mm(keys, grad_scores) * HD ** (-0.5)
            grad_mixed[h * HD : (h + 1) * HD, :] = unrotated(grad_q, rot[...]).astype(BF)
            grad_k = grad_k + mm_nt(query, grad_scores) * HD ** (-0.5)
            grad_v = grad_v + mm_nt(grad_out, soft.astype(BF))
        at = D + kv * HD
        grad_mixed[at : at + HD, :] = unrotated(grad_k, rot[...]).astype(BF)
        at = D + (KVH + kv) * HD
        grad_mixed[at : at + HD, :] = grad_v.astype(BF)
    for stream in early:
        stream.three()
    lays[2].wait()
    attn_rows = mm(lay_attn[...], grad_mixed[...]).astype(BF)
    both = jnp.concatenate([attn_rows, out_rows], 1)
    seen = jnp.concatenate([n1[...], att[...]], 1)
    parts[:, :, :, ATTN_AT:PACKED, :] = mm_nt(both, seen).astype(BF).reshape(4, 4, 2, 48, D)
    parts[:, :, :, PACKED:SUMMED, :] = jnp.zeros((4, 4, 2, SUMMED - PACKED, D), BF)
    for stream in late:
        stream.one()
    grad_normed = turned(mm_tn(attn_rows, rows48))
    part, gain1 = rms_back(h0[...], columns[:, 0:1], grad_normed)
    grad_h0 = (grad_h1 + part).astype(BF)
    grad_embedded[...] = grad_h0
    slot = lax.broadcasted_iota(jnp.int32, (NW * CAP, T), 0)
    picks = jnp.where(slot == slot_row[0:1, :], 1.0, 0.0).astype(BF)
    rows[...] = mm_nt(picks, grad_h0).astype(BF)
    give = Scatter(lambda p: rows.at[slots(p)], lambda p: rows_in.at[slots(p)], row_s, row_r, me)
    give.start()
    for stream in early:
        stream.four()
    trade.forward()
    lane = lax.broadcasted_iota(jnp.int32, (D, 128), 1)
    table = jnp.where(lane == 0, gain1, jnp.where(lane == 1, gain2, jnp.where(lane == 2, gain3, 0.0)))
    lost = jnp.sum(loss[0:1, :], 1, keepdims=True)
    table = table.T[0:8, :]
    tree = Tree(hold, land_z, land_y, land_x, tree_s, tree_r)
    tree.start(jnp.where(lax.broadcasted_iota(jnp.int32, (8, D), 0) == 3, lost, table))
    rows_in[slots(me), :] = rows[slots(me), :]
    for stream in late:
        stream.two()
    for stream in early:
        stream.five()
    tree.next(0)
    for stream in late:
        stream.three()
    for stream in late:
        stream.four()
    tree.next(1)
    for stream in early:
        stream.six()
    for stream in late:
        stream.five()
    extra_sum[...] = tree.collect(2)
    for stream in late:
        stream.six()
    for stream in streams:
        summed[stream.base : stream.base + sum(stream.sizes), :] = stream.total()
    give.wait_recv()
    trade.wait()
    for stream in streams:
        stream.finish()
    give.wait_send()
    tree.finish()
    trade.finish()


def back(grad_final, kept, packed, gains, rot, tok, slot_row, loss, head_other):
    lays = [
        jnp.asarray(spread_rows(30, 48, 0), BF),
        jnp.asarray(spread_rows(18, 48, 30), BF),
        jnp.asarray(spread_rows(18, 64, 0, 3), BF),
    ]
    return pl.pallas_call(
        back_kernel,
        name="back",
        out_shape=(
            jax.ShapeDtypeStruct((SUMMED, D), F32),
            jax.ShapeDtypeStruct((NW * CAP, D), BF),
            jax.ShapeDtypeStruct((D, SHARD), BF),
            jax.ShapeDtypeStruct((8, D), F32),
            jax.ShapeDtypeStruct((D, T), BF),
        ),
        in_specs=[VMEM] * 13 + [ANY] + [VMEM] * 5 + [ANY] * 4,
        out_specs=(VMEM, VMEM, ANY, VMEM, VMEM),
        scratch_shapes=TRUNK_SCRATCH
        + [
            pltpu.VMEM((NW * 48, QKV), BF),
            pltpu.VMEM((NW * 48, D), BF),
            pltpu.VMEM((NW * 64, D), BF),
            DMA((3,)),
            pltpu.VMEM((4, 4, 2, SUMMED, D), BF),
            pltpu.VMEM((NW * CAP, D), BF),
            pltpu.VMEM((2 * FF, T), BF),
            pltpu.VMEM((QKV, T), BF),
            pltpu.VMEM((NW * 64, T), BF),
            pltpu.VMEM((2, D // 2, SHARD), BF),
        ]
        + [DMA((NW,)), DMA((NW,)), DMA((4,)), DMA((4,))]
        + tree_scratch(D)
        + reduce_scratch(),
        compiler_params=params(5, 60),
        cost_estimate=pl.CostEstimate(flops=10**10, bytes_accessed=3 * 10**7, transcendentals=10**6),
    )(grad_final, *kept, packed, gains, rot, tok, slot_row, loss, head_other, *lays)


def adam_update(weight, grad, first, second, rate, decay):
    first = beta_one * first + (1.0 - beta_one) * grad
    second = beta_two * second + (1.0 - beta_two) * grad * grad
    ratio = first / (1.0 - beta_one**STEP) / (jnp.sqrt(second / (1.0 - beta_two**STEP)) + adam_eps)
    return (weight - rate * (ratio + decay * weight), first, second)


def adam_diff(weight, grad, first, second, anchor, rate, decay):
    return anchor - adam_update(weight, grad, first, second, rate, decay)[0]


PIECES = ((0, 0, 96), (0, 96, 96), (0, 192, 96), (1, 0, 112))


def update_kernel(
    rows, hot, head, head_in, summed, extra, gains, tm, tf, ts, ta, km, kf, ks, ka,
    table_grad, total_t, total_k, total_g, norms,
    v_rows, v_hot, v_head, v_head_in, vm, vf, vs, va, flipped,
    one_t, one_t_in, two_t, two_t_in, one_k, one_k_in, two_k, two_k_in, gains_out, gains_in,
    load_sem, one_s, one_r, two_s, two_r, three_s, three_r, gains_s, gains_r,
    hold, land_z, land_y, land_x, tree_s, tree_r,
):
    me, y, xh, z = place()
    grp = lax.axis_index("grp")
    core, x = lax.rem(grp, 2), grp // 2
    near, far = x * 2 + 1 - core, (1 - x) * 2 + core
    loads = [
        pltpu.make_async_copy(src, dst, load_sem.at[i])
        for i, (src, dst) in enumerate(
            zip((rows, hot, head, head_in, tm, tf, ts, ta), (v_rows, v_hot, v_head, v_head_in, vm, vf, vs, va))
        )
    ]
    for load in loads:
        load.start()
    barrier = pltpu.get_barrier_semaphore()
    for peer in near_peers(me, y, xh, z):
        pl.semaphore_signal(barrier, inc=1, device_id={"wide": peer}, device_id_type=MESH)
    for k in range(1, NG):
        pl.semaphore_signal(
            barrier, inc=1, device_id={"grp": lax.rem(grp + k, NG)}, device_id_type=MESH
        )
    pl.semaphore_wait(barrier, 7 + NG - 1)
    for load in loads[:4]:
        load.wait()
    for c in range(0, NW * CAP, 256):
        flipped[:, c : c + 256] = v_rows[c : c + 256, :].T
    squares = jnp.zeros((1, 256), F32)
    for c in range(0, SHARD, 256):
        part = v_head[:, c : c + 256] + v_head_in[:, c : c + 256].astype(F32)
        part = part + mm(flipped[...], v_hot[:, c : c + 256])
        table_grad[:, c : c + 256] = part
        squares = squares + jnp.sum(part * part, 0, keepdims=True)
    squares = jnp.sum(squares, 1, keepdims=True)
    trunk = jnp.sum(summed[...] * summed[...], 0, keepdims=True)
    squares = squares + jnp.sum(trunk, 1, keepdims=True)
    tree = Tree(hold, land_z, land_y, land_x, tree_s, tree_r)
    tree.start(jnp.broadcast_to(squares, (8, 128)))
    gain_grads = extra[0:3, :]
    gain_squares = jnp.sum(jnp.sum(gain_grads * gain_grads, 0, keepdims=True), 1, keepdims=True)
    tree.next(0)
    for load in loads[4:]:
        load.wait()
    tree.next(1)
    norm = jnp.sqrt(tree.collect(2)[0:1, 0:1] + gain_squares)
    factor = jnp.minimum(1.0, clip_norm / norm)
    down = lax.broadcasted_iota(jnp.int32, (8, 128), 0)
    norms[...] = jnp.where(down == 0, norm, factor)

    parts = (
        (vm, table_grad, vf, vs, va, total_t, D // 2, one_t, one_t_in, two_t, two_t_in),
        (km, summed, kf, ks, ka, total_k, SUMMED // 2, one_k, one_k_in, two_k, two_k_in),
    )
    sent = []

    def span(which, at, count, side):
        half = parts[which][6]
        return pl.ds(pl.multiple_of(side * half + at, 16), count)

    def diff(which, at, count, side):
        m, g, f, s2, a = parts[which][:5]
        rows = span(which, at, count, side)
        return adam_diff(
            m[rows, :], g[rows, :] * factor, f[rows, :], s2[rows, :], a[rows, :], inner_rate, weight_decay
        )

    for i, (which, at, count) in enumerate(PIECES):
        one, one_in = parts[which][7:9]
        rows = pl.ds(at, count)
        one[rows, :] = diff(which, at, count, 1 - core).astype(BF)
        copy = remote(one.at[rows], one_in.at[rows], one_s.at[i], one_r.at[i], grp=near)
        copy.start()
        sent.append(copy)
    for i, (which, at, count) in enumerate(PIECES):
        one, one_in, two, two_in = parts[which][7:11]
        rows = pl.ds(at, count)
        own = diff(which, at, count, core)
        sent[i].wait_recv()
        two[rows, :] = (own + one_in[rows, :].astype(F32)).astype(BF)
        copy = remote(two.at[rows], two_in.at[rows], two_s.at[i], two_r.at[i], grp=far)
        copy.start()
        sent.append(copy)
    gains_out[0:3, :] = adam_diff(
        gains[0:3, :], gain_grads * factor, gains[8:11, :], gains[16:19, :], gains[24:27, :], gain_rate, 0.0
    )
    gains_out[3:8, :] = jnp.zeros((5, D), F32)
    told = []
    for k in range(1, NG):
        to = lax.rem(grp + k, NG)
        told.append(remote(gains_out, gains_in.at[grp], gains_s.at[k], gains_r.at[grp], grp=to))
        told[-1].start()
    gains_in[grp] = gains_out[...]
    for i, (which, at, count) in enumerate(PIECES):
        total, two, two_in = parts[which][5], parts[which][9], parts[which][10]
        rows = pl.ds(at, count)
        sent[len(PIECES) + i].wait_recv()
        kept = span(which, at, count, core)
        total[kept, :] = two[rows, :].astype(F32) + two_in[rows, :].astype(F32)
        copy = remote(total.at[kept], total.at[kept], three_s.at[i], three_r.at[i], grp=near)
        copy.start()
        sent.append(copy)
    for k in range(1, NG):
        other = lax.rem(grp + k, NG)
        remote(
            gains_out, gains_in.at[other], gains_s.at[k], gains_r.at[other], grp=other
        ).wait_recv()
    total_g[...] = (gains_in[0] + gains_in[1]) + (gains_in[2] + gains_in[3])
    for i, (which, at, count) in enumerate(PIECES):
        away = parts[which][5].at[span(which, at, count, 1 - core)]
        remote(away, away, three_s.at[i], three_r.at[i], grp=near).wait_recv()
    for copy in sent + told:
        copy.wait_send()
    tree.finish()


def update(rows, hot, head, head_in, summed, extra, gains, table, trunk):
    def exchange(size, lanes):
        return [pltpu.VMEM((size // 2, lanes), BF)] * 4

    table_f32 = pltpu.VMEM((D, SHARD), F32)
    pieces = DMA((len(PIECES),))
    return pl.pallas_call(
        update_kernel,
        name="update",
        out_shape=(
            jax.ShapeDtypeStruct((D, SHARD), F32),
            jax.ShapeDtypeStruct((D, SHARD), F32),
            jax.ShapeDtypeStruct((SUMMED, D), F32),
            jax.ShapeDtypeStruct((8, D), F32),
            jax.ShapeDtypeStruct((8, 128), F32),
        ),
        in_specs=[ANY] * 4 + [VMEM] * 3 + [ANY] * 4 + [VMEM] * 4,
        out_specs=(VMEM,) * 5,
        scratch_shapes=[
            pltpu.VMEM((NW * CAP, D), BF),
            pltpu.VMEM((NW * CAP, SHARD), BF),
            table_f32,
            pltpu.VMEM((D, SHARD), BF),
            table_f32,
            table_f32,
            table_f32,
            table_f32,
            pltpu.VMEM((D, NW * CAP), BF),
        ]
        + exchange(D, SHARD)
        + exchange(SUMMED, D)
        + [pltpu.VMEM((8, D), F32), pltpu.VMEM((NG, 8, D), F32), DMA((8,))]
        + [pieces] * 6
        + [DMA((NG,)), DMA((NG,))]
        + tree_scratch(128),
        compiler_params=params(6, 48),
        cost_estimate=pl.CostEstimate(flops=2 * 10**9, bytes_accessed=3 * 10**7, transcendentals=10**6),
    )(rows, hot, head, head_in, summed, extra, gains, *table, *trunk)


def dot(spec, a, b):
    return jnp.einsum(spec, a, b, preferred_element_type=F32)


def pack(attn, ffn, proj, rows):
    down = proj[:, D:].reshape(18, 3, 512).transpose(1, 0, 2).reshape(54, 512)
    down = jnp.pad(down, ((0, 10), (0, D - 512)))
    return jnp.pad(jnp.concatenate([ffn, down, attn, proj[:, :D]], 0), ((0, rows - PACKED), (0, 0)))


def unpack(packed):
    down = packed[DOWN_AT : DOWN_AT + 54, :512].reshape(3, 18, 512).transpose(1, 0, 2).reshape(18, FF)
    proj = jnp.concatenate([packed[ATTN_AT + 30 : PACKED], down], 1)
    return packed[ATTN_AT : ATTN_AT + 30], packed[FFN_AT:DOWN_AT], proj


def on_device(
    token_ids,
    targets,
    segment_ids,
    row_counts,
    embed_table_master,
    embed_table_first,
    embed_table_second,
    embed_table_anchor,
    embed_table_momentum,
    attn_in_master,
    attn_in_first,
    attn_in_second,
    attn_in_anchor,
    attn_in_momentum,
    ffn_in_master,
    ffn_in_first,
    ffn_in_second,
    ffn_in_anchor,
    ffn_in_momentum,
    proj_out_master,
    proj_out_first,
    proj_out_second,
    proj_out_anchor,
    proj_out_momentum,
    norm_gains_master,
    norm_gains_first,
    norm_gains_second,
    norm_gains_anchor,
    norm_gains_momentum,
):
    ids = token_ids[0]
    gains = norm_gains_master[0]
    table = embed_table_master[0].T.astype(BF)
    weight = jnp.sum(row_counts[0, 0] * jnp.arange(1, 4))
    trunk = tuple(
        (attn.T, ffn.T, proj.T)
        for attn, ffn, proj in (
            (attn_in_master[0], ffn_in_master[0], proj_out_master[0]),
            (attn_in_first[0], ffn_in_first[0], proj_out_first[0]),
            (attn_in_second[0], ffn_in_second[0], proj_out_second[0]),
            (attn_in_anchor, ffn_in_anchor, proj_out_anchor),
            (attn_in_momentum, ffn_in_momentum, proj_out_momentum),
        )
    )
    packed = pack(*trunk[0], PACKED).astype(BF)
    tok = jnp.concatenate(
        [
            token_ids, targets, segment_ids, jnp.broadcast_to(weight, (1, T)), jnp.zeros((4, T), jnp.int32),
        ],
        0,
    )
    got, rows, most_all, table_other, rows_t, packed_all, picks, slot_row, hot, goals, weights = front(
        tok, table, packed
    )
    turns = (jnp.max(most_all) + CAP - 1) // CAP

    def asked_in(turn):
        ids_now = jnp.where(turn > 0, ids, 0)
        owner = ids_now // SHARD
        same = ids_now[:, None] == ids_now[None, :]
        before = jnp.arange(T)[None, :] < jnp.arange(T)[:, None]
        first_seen = ~jnp.any(same & before, 1)
        smaller = (owner[None, :] == owner[:, None]) & (ids_now[None, :] < ids_now[:, None])
        rank = jnp.sum(first_seen[None, :] & smaller, 1, dtype=jnp.int32) - turn * CAP
        slot = jnp.where((rank >= 0) & (rank < CAP), owner * CAP + rank, -1)
        chosen = jnp.arange(NW * CAP)[:, None] == slot[None, :]
        asked = jnp.max(jnp.where(chosen, (ids_now - owner * SHARD)[None, :], -1), 1).reshape(NW, 1, CAP)
        asked = jnp.pad(asked, ((0, 0), (0, 0), (0, 128 - CAP)), constant_values=-1)
        return jnp.pad(asked, ((0, 0), (0, 7), (0, 0))), chosen.astype(BF)

    def more_tokens(carry):
        turn, hidden = carry
        message, chosen = asked_in(turn)
        return turn + 1, hidden + dot("sd,st->td", more_rows(message, table), chosen)

    more = lax.while_loop(
        lambda carry: carry[0] < turns, more_tokens, (jnp.int32(1), jnp.zeros((T, D), F32))
    )[1]

    gains8 = jnp.pad(gains, ((0, 5), (0, 0)))
    rot = jnp.asarray(rope())
    final, *kept = forward(more, rows, picks, packed_all, gains8, rot, tok)
    total = weights[2, 0]
    grad_final, head_own, head_other, loss = head(final, rows_t, table, table_other, goals, weights)
    summed, rows_in, head_in, extra_sum, grad_embedded = back(
        grad_final, kept, packed_all, gains8, rot, tok, slot_row, loss, head_other
    )

    def more_table(carry):
        turn, grad = carry
        message, chosen = asked_in(turn)
        mine = dot("st,dt->sd", chosen, grad_embedded).astype(BF)
        got_now, rows_now = more_grads(message, mine)
        asked = got_now[:, 0, :CAP].reshape(NW * CAP)
        hot_now = (asked[:, None] == jnp.arange(SHARD)[None, :]).astype(BF)
        return turn + 1, grad + dot("sd,sv->dv", rows_now, hot_now)

    head_grad = lax.while_loop(lambda carry: carry[0] < turns, more_table, (jnp.int32(1), head_own))[1]
    kinds = [
        (
            embed_table_master[0].T,
            embed_table_first[0].T,
            embed_table_second[0].T,
            embed_table_anchor.T,
            embed_table_momentum.T,
        )
    ]
    kinds += [tuple(arrays[index] for arrays in trunk) for index in range(3)]
    kinds.append(
        (gains, norm_gains_first[0], norm_gains_second[0], norm_gains_anchor, norm_gains_momentum)
    )
    table_grad, total_t, total_k, total_g, norms = update(
        rows_in,
        hot,
        head_grad,
        head_in,
        summed,
        extra_sum,
        jnp.concatenate([jnp.pad(value, ((0, 5), (0, 0))) for value in kinds[4][:4]], 0),
        kinds[0][:4],
        [pack(*arrays, SUMMED) for arrays in trunk[:4]],
    )
    grads = (table_grad,) + unpack(summed) + (extra_sum[:3],)
    sums = (total_t,) + unpack(total_k) + (total_g[:3],)
    loss_total, norm, factor = extra_sum[3, 0], norms[0, 0], norms[1, 0]
    results = [loss_total.reshape(1), total.reshape(1), norm.reshape(1)]
    for index in range(5):
        _, first, second, anchor, momentum = kinds[index]
        average = sums[index] / NG
        outer = outer_momentum * momentum + average
        weight = anchor - outer_rate * (average + outer_momentum * outer)
        grad = grads[index] * factor
        first = beta_one * first + (1.0 - beta_one) * grad
        second = beta_two * second + (1.0 - beta_two) * grad * grad
        values = [average, outer, weight, first, second]
        if index < 4:
            values = [value.T for value in values]
        results += values[:3] + [values[3][None], values[4][None]]
    return tuple(results)


def solution(mesh):
    in_specs = (
        P("grp", "wide"),
        P("grp", "wide"),
        P("grp", "wide"),
        P("grp", "wide", None),
        P("grp", "wide", None),
        P("grp", "wide", None),
        P("grp", "wide", None),
        P("wide", None),
        P("wide", None),
        P("grp", None, "wide"),
        P("grp", None, "wide"),
        P("grp", None, "wide"),
        P(None, "wide"),
        P(None, "wide"),
        P("grp", None, "wide"),
        P("grp", None, "wide"),
        P("grp", None, "wide"),
        P(None, "wide"),
        P(None, "wide"),
        P("grp", None, "wide"),
        P("grp", None, "wide"),
        P("grp", None, "wide"),
        P(None, "wide"),
        P(None, "wide"),
        P("grp", None, None),
        P("grp", None, None),
        P("grp", None, None),
        P(),
        P(),
    )
    out_specs = (
        P("grp"),
        P("grp"),
        P("grp"),
        P("wide", None),
        P("wide", None),
        P("wide", None),
        P("grp", "wide", None),
        P("grp", "wide", None),
        P(None, "wide"),
        P(None, "wide"),
        P(None, "wide"),
        P("grp", None, "wide"),
        P("grp", None, "wide"),
        P(None, "wide"),
        P(None, "wide"),
        P(None, "wide"),
        P("grp", None, "wide"),
        P("grp", None, "wide"),
        P(None, "wide"),
        P(None, "wide"),
        P(None, "wide"),
        P("grp", None, "wide"),
        P("grp", None, "wide"),
        P(),
        P(),
        P(),
        P("grp", None, None),
        P("grp", None, None),
    )
    return jax.shard_map(
        on_device, mesh=mesh, in_specs=in_specs, out_specs=out_specs, check_vma=False
    )
```

profile of v0, /device:TPU:1, one launch (start us, length us, event | category | flops | bytes accessed | tf_op | source)
XLA Modules:
  0.0 419.7 jit_solution(7730735830262419988)
XLA Ops:
  0.7 0.9 copy.139
  1.6 0.1 slice.96
  1.7 0.1 reshape.211
  1.8 0.0 copy-start.30
  1.8 0.0 copy-start.31
  1.9 0.9 copy.144
  2.9 1.7 fusion.38.packed
  4.5 2.2 bitcast_convert_fusion.table
  6.8 0.6 fusion.37
  7.4 0.6 broadcast_in_dim.109
  8.1 0.6 concatenate.25.tok
  8.7 78.2 %front.1 = (s32[32,8,128]{2,1,0:T(8,128)}, bf16[1024,576]{1,0:T(8,128)(2,1)}, s32[4,8,128]{2,1,0:T(8,128)}, bf16[576,1536]{1,0:T(8,128)(2,1)}, bf16[3072,576]{1,...) custom-call(s32[8,256]{1,0:T(8,128)} %concatenate.25.tok, ...), custom_call_target="tpu_custom_call" | custom-call | flops 2000000000 | bytes 30000000 | tf_op jit(solution)/shard_map/front/pallas_call | solution.py:508
  87.0 1.4 reduce_max.33
  89.1 0.2 while.24
  89.3 1.1 copy.91.more
  90.4 0.6 pad.62.gains
  91.0 14.5 %forward.1 = (bf16[576,256]{1,0:T(8,128)(2,1)}, f32[576,256]{1,0:T(8,128)}, bf16[576,256]{1,0:T(8,128)(2,1)}, bf16[576,256]{1,0:T(8,128)(2,1)}, bf16[192,256]{1,...) custom-call(f32[256,576]{1,0:T(8,128)} %copy.91.more, ...), custom_call_target="tpu_custom_call" | custom-call | flops 4000000000 | bytes 20000000 | tf_op jit(solution)/shard_map/forward/pallas_call | solution.py:711
  105.4 120.9 %head.1 = (f32[576,256]{1,0:T(8,128)}, f32[576,1536]{1,0:T(8,128)}, bf16[576,1536]{1,0:T(8,128)(2,1)}, f32[8,256]{1,0:T(8,128)}) custom-call(bf16[576,256]{1,0:T(8,128)(2,1)} %get-tuple-element.210.final, bf16[3072,576]{1,0:T(8,128)(2,1)} %get-tuple-element.211.rows_t, bf16[576,1536]{1,0:T(8,128)(2,1)S(1)} %get-tuple-element.513, ...), custom_call_target="tpu_custom_call" | custom-call | flops 43486543872 | bytes 20000000 | tf_op jit(solution)/shard_map/head/pallas_call | solution.py:1128
  226.4 89.3 %back.1 = (f32[224,576]{1,0:T(8,128)}, bf16[1024,576]{1,0:T(8,128)(2,1)}, bf16[576,1536]{1,0:T(8,128)(2,1)}, f32[8,576]{1,0:T(8,128)}, bf16[576,256]{1,0:T(8,128)(2,1)S(1)}) custom-call(f32[576,256]{1,0:T(8,128)} %get-tuple-element.215.grad_final, f32[576,256]{1,0:T(8,128)} %get-tuple-element.216.h0, bf16[576,256]{1,0:T(8,128)(2,1)} %get-tuple-element.217.n1, ...), custom_call_target="tpu_custom_call" | custom-call | flops 10000000000 | bytes 30000000 | tf_op jit(solution)/shard_map/back/pallas_call | solution.py:1459
  315.6 0.0 copy-start.7
  315.7 0.0 copy-start.25
  315.7 0.2 while.25
  315.9 0.0 copy-start.16
  315.9 0.0 copy-start.8
  315.9 0.7 copy-done.7
  316.6 0.9 fusion.19
  317.5 0.0 copy-start.18
  317.5 0.0 copy-start.10
  317.6 0.8 copy_bitcast_fusion.8
  318.4 0.9 copy.138
  319.3 0.1 slice.98
  319.4 0.1 reshape.213
  319.8 0.1 slice.100
  319.9 0.1 reshape.215
  320.2 1.0 slice.102
  321.2 0.1 reshape.217
  321.3 0.7 reshape.218
  322.0 0.8 slice.103
  322.8 1.0 fusion.13
  323.9 1.3 copy-done.1
  325.2 65.6 %update.1 = (f32[576,1536]{1,0:T(8,128)}, f32[576,1536]{1,0:T(8,128)}, f32[224,576]{1,0:T(8,128)S(1)}, f32[8,576]{1,0:T(8,128)S(1)}, f32[8,128]{1,0:T(8,128)S(1)}) custom-call(bf16[1024,576]{1,0:T(8,128)(2,1)S(1)} %copy-done.1, bf16[1024,1536]{1,0:T(8,128)(2,1)} %get-tuple-element.233.hot, f32[576,1536]{1,0:T(8,128)} %get-tuple-element.236.head, ...), custom_call_target="tpu_custom_call" | custom-call | flops 2000000000 | bytes 30000000 | tf_op jit(solution)/shard_map/update/pallas_call | solution.py:1632
  390.8 0.5 fusion.39
  391.3 0.7 fusion.36
  392.0 0.6 copy.101
  392.6 0.6 copy.102
  393.3 0.1 copy.140
  393.4 0.1 copy.113
  393.5 1.8 fusion.25
  395.2 0.8 copy.100
  396.0 0.8 copy.99
  396.9 0.1 copy.141
  397.0 0.1 copy.112
  397.1 0.9 subtract_bitcast_fusion.2
  398.1 1.6 fusion.22
  399.7 0.7 fusion.30
  400.4 0.7 copy.97
  401.1 0.7 copy.98
  401.8 8.4 %fusion.10 = (f32[1,1536,576]{1,2,0:T(8,128)}, f32[1,1536,576]{1,2,0:T(8,128)}) fusion(f32[576,1536]{1,0:T(8,128)} %get-tuple-element.241, f32[]{:T(128)} %bitcast.37, f32[1,1536,576]{1,2,0:T(8,128)} %param.43, f32[1,1536,576]{1,2,0:T(8,128)S(1)} %copy-done.3), kind=kLoop, calls=%fused_computation.35 | loop fusion | flops 7077888 | bytes 17694724 | tf_op jit(solution)/shard_map/broadcast_in_dim | solution.py:1820
  410.3 5.3 %subtract_bitcast_fusion = (f32[1536,576]{0,1:T(8,128)}, f32[1536,576]{0,1:T(8,128)}, f32[1536,576]{0,1:T(8,128)}) fusion(f32[1536,576]{0,1:T(8,128)S(1)} %copy-done.5, f32[576,1536]{1,0:T(8,128)S(1)} %copy-done.6, f32[1536,576]{0,1:T(8,128)S(1)} %copy-done.4), kind=kLoop, calls=%fused_computation.38 | loop fusion | flops 6193152 | bytes 21233664 | tf_op jit(solution)/shard_map/transpose | solution.py:1819
  415.5 0.9 subtract_bitcast_fusion.1
  416.5 0.7 subtract_bitcast_fusion.3
  417.2 0.6 multiply_subtract_fusion.2
  417.8 0.5 slice.76
  418.3 1.2 slice.77
  (87 shorter events, 0.8 us)
Async XLA Ops:
  1.7 5.0 %copy-start.32 = (s32[1,1,3]{2,1,0:T(1,128)S(1)}, s32[1,1,3]{2,1,0:T(1,128)}, u32[]{:S(2)}) copy-start(s32[1,1,3]{2,1,0:T(1,128)} %param.40) | copy-start | bytes 40
  1.8 6.3 %copy-start.22 = (s32[1,256]{1,0:T(1,128)S(1)}, s32[1,256]{1,0:T(1,128)}, u32[]{:S(2)}) copy-start(s32[1,256]{1,0:T(1,128)} %param.37) | copy-start | bytes 3076
  1.8 6.3 %copy-start.30 = (s32[1,256]{1,0:T(1,128)S(1)}, s32[1,256]{1,0:T(1,128)}, u32[]{:S(2)}) copy-start(s32[1,256]{1,0:T(1,128)} %param.38) | copy-start | bytes 3076
  1.8 6.3 %copy-start.31 = (s32[1,256]{1,0:T(1,128)S(1)}, s32[1,256]{1,0:T(1,128)}, u32[]{:S(2)}) copy-start(s32[1,256]{1,0:T(1,128)} %param.39) | copy-start | bytes 3076
  1.9 85.0 %copy-start.14 = (f32[18,576]{1,0:T(8,128)}, f32[18,576]{1,0:T(8,128)S(1)}, u32[]{:S(2)}) copy-start(f32[18,576]{1,0:T(8,128)S(1)} %slice.97) | copy-start | bytes 124420
  89.0 1.3 copy-start.29
  315.6 0.9 copy-start.7
  315.7 1.9 copy-start.26
  315.7 2.7 copy-start.23
  315.7 2.6 copy-start.25
  315.9 3.7 copy-start.16
  315.9 3.7 copy-start.8
  315.9 3.8 copy-start.13
  317.5 2.6 copy-start.18
  317.5 2.6 copy-start.10
  319.6 3.2 copy-start.11
  319.7 4.1 copy-start
  319.8 4.1 copy-start.2
  323.9 1.3 copy-start.1
  325.2 66.1 %copy-start.27 = (f32[1,3,576]{2,0,1:T(1,128)S(1)}, f32[1,3,576]{2,0,1:T(1,128)}, u32[]{:S(2)}) copy-start(f32[1,3,576]{2,0,1:T(1,128)} %param.62) | copy-start | bytes 20740
  390.8 6.3 %copy-start.12 = (f32[2112,18]{0,1:T(8,128)S(1)}, f32[2112,18]{0,1:T(8,128)}, u32[]{:S(2)}) copy-start(f32[2112,18]{0,1:T(8,128)} %param.59) | copy-start | bytes 456196
  390.8 6.3 %copy-start.21 = (f32[2112,18]{0,1:T(8,128)S(1)}, f32[2112,18]{0,1:T(8,128)}, u32[]{:S(2)}) copy-start(f32[2112,18]{0,1:T(8,128)} %param.60) | copy-start | bytes 456196
  390.8 7.3 %copy-start.9 = (f32[1,576,96]{1,2,0:T(8,128)S(1)}, f32[1,576,96]{1,2,0:T(8,128)}, u32[]{:S(2)}) copy-start(f32[1,576,96]{1,2,0:T(8,128)} %param.52) | copy-start | bytes 663556
  393.2 6.5 %copy-start.17 = (f32[1,576,30]{1,0,2:T(1,128)S(1)}, f32[1,576,30]{1,0,2:T(1,128)}, u32[]{:S(2)}) copy-start(f32[1,576,30]{1,0,2:T(1,128)} %param.47) | copy-start | bytes 207364
  393.2 6.5 %copy-start.19 = (f32[1,576,30]{1,0,2:T(1,128)S(1)}, f32[1,576,30]{1,0,2:T(1,128)}, u32[]{:S(2)}) copy-start(f32[1,576,30]{1,0,2:T(1,128)} %param.48) | copy-start | bytes 207364
  396.9 4.9 %copy-start.3 = (f32[1,1536,576]{1,2,0:T(8,128)S(1)}, f32[1,1536,576]{1,2,0:T(8,128)}, u32[]{:S(2)}) copy-start(f32[1,1536,576]{1,2,0:T(8,128)} %param.42) | copy-start | bytes 10616836
  401.8 8.4 %copy-start.4 = (f32[1536,576]{0,1:T(8,128)S(1)}, f32[1536,576]{0,1:T(8,128)}, u32[]{:S(2)}) copy-start(f32[1536,576]{0,1:T(8,128)} %param.44) | copy-start | bytes 10616836
  401.8 8.4 %copy-start.5 = (f32[1536,576]{0,1:T(8,128)S(1)}, f32[1536,576]{0,1:T(8,128)}, u32[]{:S(2)}) copy-start(f32[1536,576]{0,1:T(8,128)} %param.45) | copy-start | bytes 10616836
  401.8 8.4 %copy-start.6 = (f32[576,1536]{1,0:T(8,128)S(1)}, f32[576,1536]{1,0:T(8,128)}, u32[]{:S(2)}) copy-start(f32[576,1536]{1,0:T(8,128)} %get-tuple-element.240) | copy-start | bytes 10616836
  410.2 5.3 %copy-start.20 = (f32[576,96]{0,1:T(8,128)S(1)}, f32[576,96]{0,1:T(8,128)}, u32[]{:S(2)}) copy-start(f32[576,96]{0,1:T(8,128)} %param.55) | copy-start | bytes 663556
  410.2 6.2 %copy-start.15 = (f32[576,30]{0,1:T(8,128)S(1)}, f32[576,30]{0,1:T(8,128)}, u32[]{:S(2)}) copy-start(f32[576,30]{0,1:T(8,128)} %param.49) | copy-start | bytes 207364
  410.2 6.2 %copy-start.24 = (f32[576,30]{0,1:T(8,128)S(1)}, f32[576,30]{0,1:T(8,128)}, u32[]{:S(2)}) copy-start(f32[576,30]{0,1:T(8,128)} %param.50) | copy-start | bytes 207364
  410.3 6.9 %copy-start.28 = (f32[3,576]{1,0:T(4,128)S(1)}, f32[3,576]{1,0:T(4,128)}, u32[]{:S(2)}) copy-start(f32[3,576]{1,0:T(4,128)} %param.65) | copy-start | bytes 20740
where the time goes:
time: 428 us; the launch traced here: 420 us
  Pallas kernels  368 us (86%)
  other arithmetic  29.4 us (7%)
  local copies, waits for them, and re-layouts  19.1 us (4%)
    pallas_call x1, Pallas kernels, head(): pl.pallas_call(head_kernel, name='head', out_shape=(jax.ShapeDtypeStruct(...  121 us
    pallas_call x1, Pallas kernels, back(): pl.pallas_call(back_kernel, name='back', out_shape=(jax.ShapeDtypeStruct(...  89.3 us
    pallas_call x1, Pallas kernels, front(): pl.pallas_call(front_kernel, name='front', out_shape=(jax.ShapeDtypeStruc...  78.2 us
    pallas_call x1, Pallas kernels, update(): pl.pallas_call(update_kernel, name='update', out_shape=(jax.ShapeDtypeStr...  65.6 us
    pallas_call x1, Pallas kernels, forward(): pl.pallas_call(forward_kernel, name='forward', out_shape=(out(D, BF), out...  14.5 us
    broadcast_in_dim x5, other arithmetic, on_device(): results += values[:3] + [values[3][None], values[4][None]]  13.1 us
    unnamed x84, local copies, waits for them, and re-layouts  10.2 us

commit v1 on v0

--- a/solution.py
+++ b/solution.py
@@ -402,7 +402,7 @@
     lanes = lax.broadcasted_iota(jnp.int32, (CAP, SHARD), 1).astype(F32)
     for d in range(NW):
         hot[d * CAP : (d + 1) * CAP, :] = jnp.where(lanes == mine[:, d : d + 1], 1.0, 0.0).astype(BF)
-    step = 8 * CAP
+    step = 16 * CAP
     for first in range(0, NW * CAP, step):
         picked = lax.dot_general(
             hot[first : first + step, :], table[...], (((1,), (1,)), ((), ())), preferred_element_type=F32
@@ -796,10 +796,18 @@
     return pl.ds(pl.multiple_of(j * T, T), T)
 
 
+def pair_cols(p):
+    return pl.ds(pl.multiple_of(p * 2 * T, 2 * T), 2 * T)
+
+
+def side_by_side(ref, p, rows):
+    return jnp.concatenate([ref[2 * p, rows, :], ref[2 * p + 1, rows, :]], 1)
+
+
 def head_kernel(
     final, rows_t, table, table_other, goal, weights,
     grad_final, head_own, head_other, loss,
-    fall, expo, even, odd_grad, tops, stat, stat_in, coef, coef_in, parts,
+    fall, expo, tops, stat, stat_in, coef, coef_in, parts,
     part_a, part_b, whole_a, whole_b, sum_a, sum_b, part_a2, part_b2, whole_a2, whole_b2,
     g_s, g_r, st_s, st_r, co_s, co_r, a_s, b_s, pa_r, pb_r, wa_r, wb_r, a2_s, b2_s, a2_r, b2_r,
 ):
@@ -839,30 +847,29 @@
     ring.own(final, fall.at[:, cols(mine)], 0)
     fall[:, cols(mine)] = final[...]
 
-    def logits(j):
-        seen = fall[:, cols(j)]
-        goals = goal[j]
-        group, hit = goals >> 3, jnp.zeros((8, T), F32)
+    def logits(p):
+        seen = fall[:, pair_cols(p)]
+        goals = side_by_side(goal, p, slice(0, 8))
+        group, hit = goals >> 3, jnp.zeros((8, 2 * T), F32)
         tip, weight = [], []
-        ahead = mm(rows_t[0:CH, :], seen)
         for c in range(NCH):
-            part = ahead
-            if c + 1 < NCH:
-                ahead = mm(rows_t[(c + 1) * CH : (c + 2) * CH, :], seen)
+            part = mm(rows_t[c * CH : (c + 1) * CH, :], seen)
             top = jnp.max(part, 0, keepdims=True)
             power = jnp.exp(part - top)
             for r in range(CH // 8):
                 hit = jnp.where(group == c * (CH // 8) + r, part[8 * r : 8 * r + 8, :], hit)
-            expo[c * CH : (c + 1) * CH, cols(j)] = power.astype(BF)
+            expo[c * CH : (c + 1) * CH, pair_cols(p)] = power.astype(BF)
             tip.append(top)
             weight.append(jnp.sum(power, 0, keepdims=True))
-        spot = lax.broadcasted_iota(jnp.int32, (8, T), 0)
+        spot = lax.broadcasted_iota(jnp.int32, (8, 2 * T), 0)
         hit = jnp.sum(jnp.where(spot == (goals & 7), hit, 0.0), 0, keepdims=True)
         top = functools.reduce(jnp.maximum, tip)
         total = sum(w * jnp.exp(t - top) for w, t in zip(weight, tip))
-        zero = jnp.zeros((1, T), F32)
-        tops[j] = jnp.concatenate(tip + [zero] * (8 - NCH), 0)
-        stat[j] = jnp.concatenate([top, total, hit] + [zero] * 5, 0)
+        zero = jnp.zeros((1, 2 * T), F32)
+        tops[p] = jnp.concatenate(tip + [zero] * (8 - NCH), 0)
+        stats = jnp.concatenate([top, total, hit] + [zero] * 5, 0)
+        stat[2 * p] = stats[:, 0:T]
+        stat[2 * p + 1] = stats[:, T : 2 * T]
 
     def tell(j):
         return remote(stat.at[j], stat_in.at[mine], st_s.at[j], st_r.at[mine], wide=dev(j))
@@ -870,34 +877,41 @@
     def block(dy, dz):
         return turn4(y, dy) * 4 + turn4(z, dz)
 
-    def forward(offsets):
+    half = z // 2
+
+    def pair(dy, away):
+        return turn4(y, dy) * 2 + lax.rem(half + away, 2)
+
+    def forward(at):
         def one(k, carry):
-            j = block(*offsets(k))
-            logits(j)
-            tell(j).start()
+            p = pair(*at(k))
+            logits(p)
+            tell(2 * p).start()
+            tell(2 * p + 1).start()
             return carry
 
         return one
 
-    def odd(k):
-        return 1 + 2 * lax.rem(k, 2)
-
-    logits(mine)
+    ring.near()
+    logits(pair(0, 0))
     stat_in[mine] = stat[mine]
-    ring.near()
-    lax.fori_loop(0, 4, forward(lambda k: ((1 - k // 2) * odd(k), (k // 2) * odd(k))), 0)
+    tell(2 * (mine // 2) + 1 - lax.rem(mine, 2)).start()
     ring.far()
-    lax.fori_loop(0, 2, forward(lambda k: (2 * (1 - k), 2 * k)), 0)
+    forward(lambda k: (0, 1))(0, 0)
     ring.cross()
-    lax.fori_loop(0, 4, forward(lambda k: (odd(k // 2), odd(k))), 0)
+    lax.fori_loop(0, 2, forward(lambda k: (1 + 2 * k, 0)), 0)
     ring.last()
     lax.fori_loop(
         0,
         4,
-        forward(lambda k: (2 * (1 - k // 2) + odd(k) * (k // 2), odd(k) * (1 - k // 2) + 2 * (k // 2))),
+        forward(
+            lambda k: (
+                (1 + 2 * lax.rem(k, 2)) * (1 - k // 2) + 2 * (k // 2),
+                1 - (k // 2) * (1 - lax.rem(k, 2)),
+            )
+        ),
         0,
     )
-    forward(lambda k: (2, 2))(0, 0)
 
     def hear(k, carry):
         j = lax.rem(mine + k, 16)
@@ -961,109 +975,90 @@
             b_s.at[j, 0], wb_r.at[index, column], wide=y_to[(up, down)[index]],
         )
 
-    def offsets(k):
-        return lax.rem(2 + k // 4, 4), lax.rem(2 + k, 4)
+    def pair_at(k):
+        return pair(lax.rem(2 + k // 2, 4), lax.rem(k + 1, 2))
 
     def post(k):
-        dy, dz = offsets(k)
-        j = block(dy, dz)
-
-        @pl.when(dz == 2)
+        p = pair_at(k)
+        for j in (2 * p, 2 * p + 1):
+            dy, dz = lax.rem(j // 4 - y + 4, 4), lax.rem(lax.rem(j, 4) - z + 4, 4)
+
+            @pl.when(dz == 2)
+            def _(j=j):
+                piece_a(j, 0).start()
+                piece_a(j, 1).start()
+
+            @pl.when(dy == 2)
+            def _(j=j):
+                piece_b(j, 0).start()
+                piece_b(j, 1).start()
+
+        for j in (2 * p, 2 * p + 1):
+            dy, dz = lax.rem(j // 4 - y + 4, 4), lax.rem(lax.rem(j, 4) - z + 4, 4)
+            for index, step in enumerate((up, down)):
+
+                @pl.when(dz == step)
+                def _(j=j, index=index):
+                    row = j // 4
+                    arrived(part_a.at[index, row], pa_r.at[index, row])
+                    rows = pl.ds(index * QUART, QUART)
+                    total = parts[j, rows, :].astype(F32) + part_a[index, row].astype(F32)
+                    parts[j, rows, :] = total.astype(BF)
+                    half_a(j, index).start()
+
+                @pl.when(dy == step)
+                def _(j=j, index=index):
+                    column = lax.rem(j, 4)
+                    arrived(part_b.at[index, column], pb_r.at[index, column])
+                    rows = pl.ds((2 + index) * QUART, QUART)
+                    total = parts[j, rows, :].astype(F32) + part_b[index, column].astype(F32)
+                    parts[j, rows, :] = total.astype(BF)
+                    half_b(j, index).start()
+
+    def backward(k, carry):
+        p = pair_at(k)
+        for j in (2 * p, 2 * p + 1):
+
+            @pl.when(j != mine)
+            def _(j=j):
+                arrived(coef_in.at[j], co_r.at[j])
+
+        lse, soft, pick = (side_by_side(coef_in, p, slice(i, i + 1)) for i in range(3))
+        goals = side_by_side(goal, p, slice(0, 8))
+        group = goals >> 3
+        pick = jnp.where(lax.broadcasted_iota(jnp.int32, (8, 2 * T), 0) == (goals & 7), pick, 0.0)
+        for c in range(NCH):
+            scale = soft * jnp.exp(tops[p, c : c + 1, :] - lse)
+            power = expo[c * CH : (c + 1) * CH, pair_cols(p)].astype(F32)
+            spot = lax.broadcasted_iota(jnp.int32, (CH // 8, 8, 2 * T), 0) + c * (CH // 8)
+            drop = jnp.where(spot == group[None], pick[None], 0.0).reshape(CH, 2 * T)
+            expo[c * CH : (c + 1) * CH, pair_cols(p)] = (power * scale - drop).astype(BF)
+        product = mm(table[...], expo[0:SHARD, pair_cols(p)])
+        product += mm(table_other[...], expo[SHARD:VOC, pair_cols(p)])
+        parts[2 * p] = product[:, 0:T].astype(BF)
+        parts[2 * p + 1] = product[:, T : 2 * T].astype(BF)
+
+        @pl.when(k > 0)
         def _():
-            piece_a(j, 0).start()
-            piece_a(j, 1).start()
-
-        @pl.when(dy == 2)
-        def _():
-            piece_b(j, 0).start()
-            piece_b(j, 1).start()
-
-        for index, step in enumerate((up, down)):
-
-            @pl.when(dz == step)
-            def _():
-                row = j // 4
-                arrived(part_a.at[index, row], pa_r.at[index, row])
-                rows = pl.ds(index * QUART, QUART)
-                total = parts[j, rows, :].astype(F32) + part_a[index, row].astype(F32)
-                parts[j, rows, :] = total.astype(BF)
-                half_a(j, index).start()
-
-            @pl.when(dy == step)
-            def _():
-                column = lax.rem(j, 4)
-                arrived(part_b.at[index, column], pb_r.at[index, column])
-                rows = pl.ds((2 + index) * QUART, QUART)
-                total = parts[j, rows, :].astype(F32) + part_b[index, column].astype(F32)
-                parts[j, rows, :] = total.astype(BF)
-                half_b(j, index).start()
-
-    def await_coef(k):
-        j = block(*offsets(k))
-
-        @pl.when(k != 10)
-        def _():
-            arrived(coef_in.at[j], co_r.at[j])
-
-    def grad_logits(k, out):
-        j = block(*offsets(k))
-        lse, soft, pick = coef_in[j, 0:1, :], coef_in[j, 1:2, :], coef_in[j, 2:3, :]
-        goals = goal[j]
-        group = goals >> 3
-        pick = jnp.where(lax.broadcasted_iota(jnp.int32, (8, T), 0) == (goals & 7), pick, 0.0)
-        for c in range(NCH):
-            scale = soft * jnp.exp(tops[j, c : c + 1, :] - lse)
-            power = expo[c * CH : (c + 1) * CH, cols(j)].astype(F32)
-            spot = lax.broadcasted_iota(jnp.int32, (CH // 8, 8, T), 0) + c * (CH // 8)
-            drop = jnp.where(spot == group[None], pick[None], 0.0).reshape(CH, T)
-            grad = (power * scale - drop).astype(BF)
-            out[c * CH : (c + 1) * CH, :] = grad
-            expo[c * CH : (c + 1) * CH, cols(j)] = grad
-
-    def to_tokens(k, grad):
-        product = mm(table[...], grad[0:SHARD, :]) + mm(table_other[...], grad[SHARD:VOC, :])
-        parts[block(*offsets(k))] = product.astype(BF)
-
-    def backward(i, carry):
-        for k, now, ahead in ((2 * i, even, odd_grad), (2 * i + 1, odd_grad, even)):
-            await_coef(k + 1)
-            to_tokens(k, now)
-            grad_logits(k + 1, ahead)
-
-            @pl.when(k > 0)
-            def _():
-                post(k - 1)
+            post(k - 1)
 
         return carry
 
-    await_coef(0)
-    grad_logits(0, even)
-    lax.fori_loop(0, 7, backward, 0)
-    await_coef(15)
-    to_tokens(14, even)
-    grad_logits(15, odd_grad)
-    post(13)
-    to_tokens(15, odd_grad)
-    post(14)
-    post(15)
+    lax.fori_loop(0, 8, backward, 0)
+    post(7)
 
     def head_chunk(c):
-        return lax.dot_general(
-            fall[...],
-            expo[pl.ds(pl.multiple_of(c * 256, 256), 256), :],
-            (((1,), (1,)), ((), ())),
-            preferred_element_type=F32,
-        )
+        return mm_nt(fall[...], expo[pl.ds(pl.multiple_of(c * 512, 512), 512), :])
 
     def other_chunk(c, carry):
-        head_other[:, cols(c)] = head_chunk(c + SHARD // 256).astype(BF)
+        head_other[:, pair_cols(c)] = head_chunk(c + SHARD // 512).astype(BF)
         return carry
 
     def own_chunk(c, carry):
-        head_own[:, cols(c)] = head_chunk(c)
+        head_own[:, pair_cols(c)] = head_chunk(c)
         return carry
 
-    lax.fori_loop(0, SHARD // 256, other_chunk, 0)
+    lax.fori_loop(0, SHARD // 512, other_chunk, 0)
 
     kinds = (
         (whole_a, wa_r, sum_a, part_a2, whole_a2, a2_s, a2_r, y_to, 0),
@@ -1085,7 +1080,7 @@
                 for index, step in enumerate((up, down)):
                     piece = total.at[1, pl.ds(index * QUART, QUART)]
                     send(piece, part2.at[index], s2.at[index], r2.at[index], to[step])
-    lax.fori_loop(0, SHARD // 512, own_chunk, 0)
+    lax.fori_loop(0, 2, own_chunk, 0)
     for kind, (whole, w_r, total, part2, whole2, s2, r2, to, base) in enumerate(kinds):
         for index, step in enumerate((up, down)):
             arrived(part2.at[index], r2.at[index])
@@ -1093,7 +1088,7 @@
             added = total[step - 1, rows, :].astype(F32) + part2[index].astype(F32)
             total[step - 1, rows, :] = added.astype(BF)
             send(total.at[step - 1], whole2.at[index], s2.at[2 + index], r2.at[2 + index], to[step])
-    lax.fori_loop(SHARD // 512, SHARD // 256, own_chunk, 0)
+    lax.fori_loop(2, SHARD // 512, own_chunk, 0)
     for kind, (whole, w_r, total, part2, whole2, s2, r2, to, base) in enumerate(kinds):
         for index in range(2):
             arrived(whole2.at[index], r2.at[2 + index])
@@ -1139,9 +1134,7 @@
         scratch_shapes=[
             pltpu.VMEM((D, TOK), BF),
             pltpu.VMEM((VOC, TOK), BF),
-            pltpu.VMEM((VOC, T), BF),
-            pltpu.VMEM((VOC, T), BF),
-            pltpu.VMEM((16, 8, T), F32),
+            pltpu.VMEM((8, 8, 2 * T), F32),
             pltpu.VMEM((16, 8, T), F32),
             pltpu.VMEM((16, 8, T), F32),
             pltpu.VMEM((8, T), F32),
@@ -1535,11 +1528,11 @@
         load.wait()
     for c in range(0, NW * CAP, 256):
         flipped[:, c : c + 256] = v_rows[c : c + 256, :].T
-    squares = jnp.zeros((1, 256), F32)
-    for c in range(0, SHARD, 256):
-        part = v_head[:, c : c + 256] + v_head_in[:, c : c + 256].astype(F32)
-        part = part + mm(flipped[...], v_hot[:, c : c + 256])
-        table_grad[:, c : c + 256] = part
+    squares = jnp.zeros((1, 512), F32)
+    for c in range(0, SHARD, 512):
+        part = v_head[:, c : c + 512] + v_head_in[:, c : c + 512].astype(F32)
+        part = part + mm(flipped[...], v_hot[:, c : c + 512])
+        table_grad[:, c : c + 512] = part
         squares = squares + jnp.sum(part * part, 0, keepdims=True)
     squares = jnp.sum(squares, 1, keepdims=True)
     trunk = jnp.sum(summed[...] * summed[...], 0, keepdims=True)

time: 428 us -> 419 us (0.979)
  Pallas kernels: 368 us -> 360 us
    pallas_call x1, Pallas kernels: 121 us -> 113 us  [head(): pl.pallas_call(head_kernel, name='head', out_shape=(jax.ShapeDtypeStruct(...]
where the time goes in v1:
time: 419 us; the launch traced here: 411 us
  Pallas kernels  360 us (86%)
  other arithmetic  29.4 us (7%)
  local copies, waits for them, and re-layouts  19.1 us (5%)
    pallas_call x1, Pallas kernels, head(): pl.pallas_call(head_kernel, name='head', out_shape=(jax.ShapeDtypeStruct(...  113 us
    pallas_call x1, Pallas kernels, back(): pl.pallas_call(back_kernel, name='back', out_shape=(jax.ShapeDtypeStruct(...  90 us
    pallas_call x1, Pallas kernels, front(): pl.pallas_call(front_kernel, name='front', out_shape=(jax.ShapeDtypeStruc...  78.2 us
    pallas_call x1, Pallas kernels, update(): pl.pallas_call(update_kernel, name='update', out_shape=(jax.ShapeDtypeStr...  64.6 us
    pallas_call x1, Pallas kernels, forward(): pl.pallas_call(forward_kernel, name='forward', out_shape=(out(D, BF), out...  14.5 us
    broadcast_in_dim x5, other arithmetic, on_device(): results += values[:3] + [values[3][None], values[4][None]]  13.1 us
    unnamed x84, local copies, waits for them, and re-layouts  10.2 us

profile of v1, /device:TPU:1, one launch (start us, length us, event | category | flops | bytes accessed | tf_op | source)
XLA Modules:
  0.0 411.1 jit_solution(371988421250067111)
XLA Ops:
  0.7 0.9 copy.139
  1.6 0.1 slice.96
  1.7 0.0 copy-start.32
  1.7 0.1 reshape.211
  1.8 0.0 copy-start.22
  1.9 0.0 copy-start.14
  1.9 0.9 copy.144
  2.9 1.7 fusion.38.packed
  4.5 2.2 bitcast_convert_fusion.table
  6.8 0.6 fusion.37
  7.4 0.6 broadcast_in_dim.109
  8.1 0.6 concatenate.25.tok
  8.7 78.2 %front.1 = (s32[32,8,128]{2,1,0:T(8,128)}, bf16[1024,576]{1,0:T(8,128)(2,1)}, s32[4,8,128]{2,1,0:T(8,128)}, bf16[576,1536]{1,0:T(8,128)(2,1)}, bf16[3072,576]{1,...) custom-call(s32[8,256]{1,0:T(8,128)} %concatenate.25.tok, ...), custom_call_target="tpu_custom_call" | custom-call | flops 2000000000 | bytes 30000000 | tf_op jit(solution)/shard_map/front/pallas_call | solution.py:508
  87.0 1.4 reduce_max.33
  89.0 0.0 copy-start.29
  89.1 0.2 while.24
  89.3 1.1 copy.91.more
  90.4 0.6 pad.62.gains
  91.0 14.5 %forward.1 = (bf16[576,256]{1,0:T(8,128)(2,1)}, f32[576,256]{1,0:T(8,128)}, bf16[576,256]{1,0:T(8,128)(2,1)}, bf16[576,256]{1,0:T(8,128)(2,1)}, bf16[192,256]{1,...) custom-call(f32[256,576]{1,0:T(8,128)} %copy.91.more, ...), custom_call_target="tpu_custom_call" | custom-call | flops 4000000000 | bytes 20000000 | tf_op jit(solution)/shard_map/forward/pallas_call | solution.py:711
  105.4 112.6 %head.1 = (f32[576,256]{1,0:T(8,128)}, f32[576,1536]{1,0:T(8,128)}, bf16[576,1536]{1,0:T(8,128)(2,1)}, f32[8,256]{1,0:T(8,128)}) custom-call(bf16[576,256]{1,0:T(8,128)(2,1)} %get-tuple-element.210.final, bf16[3072,576]{1,0:T(8,128)(2,1)} %get-tuple-element.211.rows_t, bf16[576,1536]{1,0:T(8,128)(2,1)S(1)} %get-tuple-element.513, ...), custom_call_target="tpu_custom_call" | custom-call | flops 43486543872 | bytes 20000000 | tf_op jit(solution)/shard_map/head/pallas_call | solution.py:1123
  218.1 90.0 %back.1 = (f32[224,576]{1,0:T(8,128)}, bf16[1024,576]{1,0:T(8,128)(2,1)}, bf16[576,1536]{1,0:T(8,128)(2,1)}, f32[8,576]{1,0:T(8,128)}, bf16[576,256]{1,0:T(8,128)(2,1)S(1)}) custom-call(f32[576,256]{1,0:T(8,128)} %get-tuple-element.215.grad_final, f32[576,256]{1,0:T(8,128)} %get-tuple-element.216.h0, bf16[576,256]{1,0:T(8,128)(2,1)} %get-tuple-element.217.n1, ...), custom_call_target="tpu_custom_call" | custom-call | flops 10000000000 | bytes 30000000 | tf_op jit(solution)/shard_map/back/pallas_call | solution.py:1452
  308.1 0.0 copy-start.7
  308.1 0.0 copy-start.25
  308.1 0.2 while.25
  308.3 0.0 copy-start.16
  308.3 0.0 copy-start.8
  308.3 0.7 copy-done.7
  309.0 0.9 fusion.19
  310.0 0.8 copy_bitcast_fusion.8
  310.8 0.9 copy.138
  311.7 0.1 slice.98
  311.8 0.1 reshape.213
  312.2 0.1 slice.100
  312.3 0.1 reshape.215
  312.6 1.0 slice.102
  313.6 0.1 reshape.217
  313.7 0.7 reshape.218
  314.4 0.8 slice.103
  315.2 1.0 fusion.13
  316.3 1.3 copy-done.1
  317.6 64.6 %update.1 = (f32[576,1536]{1,0:T(8,128)}, f32[576,1536]{1,0:T(8,128)}, f32[224,576]{1,0:T(8,128)S(1)}, f32[8,576]{1,0:T(8,128)S(1)}, f32[8,128]{1,0:T(8,128)S(1)}) custom-call(bf16[1024,576]{1,0:T(8,128)(2,1)S(1)} %copy-done.1, bf16[1024,1536]{1,0:T(8,128)(2,1)} %get-tuple-element.233.hot, f32[576,1536]{1,0:T(8,128)} %get-tuple-element.236.head, ...), custom_call_target="tpu_custom_call" | custom-call | flops 2000000000 | bytes 30000000 | tf_op jit(solution)/shard_map/update/pallas_call | solution.py:1625
  382.3 0.5 fusion.39
  382.8 0.7 fusion.36
  383.4 0.6 copy.101
  384.0 0.6 copy.102
  384.7 0.1 copy.140
  384.8 0.1 copy.113
  384.9 1.8 fusion.25
  386.7 0.8 copy.100
  387.5 0.8 copy.99
  388.4 0.1 copy.141
  388.5 0.1 copy.112
  388.6 0.9 subtract_bitcast_fusion.2
  389.5 1.6 fusion.22
  391.2 0.7 fusion.30
  391.8 0.7 copy.97
  392.6 0.7 copy.98
  393.3 8.4 %fusion.10 = (f32[1,1536,576]{1,2,0:T(8,128)}, f32[1,1536,576]{1,2,0:T(8,128)}) fusion(f32[576,1536]{1,0:T(8,128)} %get-tuple-element.241, f32[]{:T(128)} %bitcast.37, f32[1,1536,576]{1,2,0:T(8,128)} %param.43, f32[1,1536,576]{1,2,0:T(8,128)S(1)} %copy-done.3), kind=kLoop, calls=%fused_computation.35 | loop fusion | flops 7077888 | bytes 17694724 | tf_op jit(solution)/shard_map/broadcast_in_dim | solution.py:1813
  401.7 5.3 %subtract_bitcast_fusion = (f32[1536,576]{0,1:T(8,128)}, f32[1536,576]{0,1:T(8,128)}, f32[1536,576]{0,1:T(8,128)}) fusion(f32[1536,576]{0,1:T(8,128)S(1)} %copy-done.5, f32[576,1536]{1,0:T(8,128)S(1)} %copy-done.6, f32[1536,576]{0,1:T(8,128)S(1)} %copy-done.4), kind=kLoop, calls=%fused_computation.38 | loop fusion | flops 6193152 | bytes 21233664 | tf_op jit(solution)/shard_map/transpose | solution.py:1812
  407.0 0.9 subtract_bitcast_fusion.1
  407.9 0.7 subtract_bitcast_fusion.3
  408.6 0.6 multiply_subtract_fusion.2
  409.2 0.5 slice.76
  409.8 1.2 slice.77
  (87 shorter events, 0.8 us)
Async XLA Ops:
  1.7 5.0 %copy-start.32 = (s32[1,1,3]{2,1,0:T(1,128)S(1)}, s32[1,1,3]{2,1,0:T(1,128)}, u32[]{:S(2)}) copy-start(s32[1,1,3]{2,1,0:T(1,128)} %param.40) | copy-start | bytes 40
  1.8 6.3 %copy-start.22 = (s32[1,256]{1,0:T(1,128)S(1)}, s32[1,256]{1,0:T(1,128)}, u32[]{:S(2)}) copy-start(s32[1,256]{1,0:T(1,128)} %param.37) | copy-start | bytes 3076
  1.8 6.3 %copy-start.30 = (s32[1,256]{1,0:T(1,128)S(1)}, s32[1,256]{1,0:T(1,128)}, u32[]{:S(2)}) copy-start(s32[1,256]{1,0:T(1,128)} %param.38) | copy-start | bytes 3076
  1.8 6.3 %copy-start.31 = (s32[1,256]{1,0:T(1,128)S(1)}, s32[1,256]{1,0:T(1,128)}, u32[]{:S(2)}) copy-start(s32[1,256]{1,0:T(1,128)} %param.39) | copy-start | bytes 3076
  1.9 85.0 %copy-start.14 = (f32[18,576]{1,0:T(8,128)}, f32[18,576]{1,0:T(8,128)S(1)}, u32[]{:S(2)}) copy-start(f32[18,576]{1,0:T(8,128)S(1)} %slice.97) | copy-start | bytes 124420
  89.0 1.3 copy-start.29
  308.1 0.9 copy-start.7
  308.1 1.9 copy-start.26
  308.1 2.7 copy-start.23
  308.1 2.6 copy-start.25
  308.3 3.7 copy-start.16
  308.3 3.7 copy-start.8
  308.3 3.8 copy-start.13
  309.9 2.6 copy-start.18
  309.9 2.6 copy-start.10
  312.0 3.2 copy-start.11
  312.2 4.1 %copy-start = (f32[224,576]{1,0:T(8,128)S(1)}, f32[224,576]{1,0:T(8,128)}, u32[]{:S(2)}) copy-start(f32[224,576]{1,0:T(8,128)} %get-tuple-element.238.summed) | copy-start | bytes 1548292
  312.2 4.1 %copy-start.2 = (f32[8,576]{1,0:T(8,128)S(1)}, f32[8,576]{1,0:T(8,128)}, u32[]{:S(2)}) copy-start(f32[8,576]{1,0:T(8,128)} %get-tuple-element.231.extra) | copy-start | bytes 55300
  316.3 1.3 copy-start.1
  317.6 65.2 %copy-start.27 = (f32[1,3,576]{2,0,1:T(1,128)S(1)}, f32[1,3,576]{2,0,1:T(1,128)}, u32[]{:S(2)}) copy-start(f32[1,3,576]{2,0,1:T(1,128)} %param.62) | copy-start | bytes 20740
  382.2 6.3 %copy-start.12 = (f32[2112,18]{0,1:T(8,128)S(1)}, f32[2112,18]{0,1:T(8,128)}, u32[]{:S(2)}) copy-start(f32[2112,18]{0,1:T(8,128)} %param.59) | copy-start | bytes 456196
  382.2 6.3 %copy-start.21 = (f32[2112,18]{0,1:T(8,128)S(1)}, f32[2112,18]{0,1:T(8,128)}, u32[]{:S(2)}) copy-start(f32[2112,18]{0,1:T(8,128)} %param.60) | copy-start | bytes 456196
  382.2 7.3 %copy-start.9 = (f32[1,576,96]{1,2,0:T(8,128)S(1)}, f32[1,576,96]{1,2,0:T(8,128)}, u32[]{:S(2)}) copy-start(f32[1,576,96]{1,2,0:T(8,128)} %param.52) | copy-start | bytes 663556
  384.7 6.5 %copy-start.17 = (f32[1,576,30]{1,0,2:T(1,128)S(1)}, f32[1,576,30]{1,0,2:T(1,128)}, u32[]{:S(2)}) copy-start(f32[1,576,30]{1,0,2:T(1,128)} %param.47) | copy-start | bytes 207364
  384.7 6.5 %copy-start.19 = (f32[1,576,30]{1,0,2:T(1,128)S(1)}, f32[1,576,30]{1,0,2:T(1,128)}, u32[]{:S(2)}) copy-start(f32[1,576,30]{1,0,2:T(1,128)} %param.48) | copy-start | bytes 207364
  388.4 4.9 %copy-start.3 = (f32[1,1536,576]{1,2,0:T(8,128)S(1)}, f32[1,1536,576]{1,2,0:T(8,128)}, u32[]{:S(2)}) copy-start(f32[1,1536,576]{1,2,0:T(8,128)} %param.42) | copy-start | bytes 10616836
  393.3 8.4 %copy-start.4 = (f32[1536,576]{0,1:T(8,128)S(1)}, f32[1536,576]{0,1:T(8,128)}, u32[]{:S(2)}) copy-start(f32[1536,576]{0,1:T(8,128)} %param.44) | copy-start | bytes 10616836
  393.3 8.4 %copy-start.5 = (f32[1536,576]{0,1:T(8,128)S(1)}, f32[1536,576]{0,1:T(8,128)}, u32[]{:S(2)}) copy-start(f32[1536,576]{0,1:T(8,128)} %param.45) | copy-start | bytes 10616836
  393.3 8.4 %copy-start.6 = (f32[576,1536]{1,0:T(8,128)S(1)}, f32[576,1536]{1,0:T(8,128)}, u32[]{:S(2)}) copy-start(f32[576,1536]{1,0:T(8,128)} %get-tuple-element.240) | copy-start | bytes 10616836
  401.7 5.3 %copy-start.20 = (f32[576,96]{0,1:T(8,128)S(1)}, f32[576,96]{0,1:T(8,128)}, u32[]{:S(2)}) copy-start(f32[576,96]{0,1:T(8,128)} %param.55) | copy-start | bytes 663556
  401.7 6.2 %copy-start.15 = (f32[576,30]{0,1:T(8,128)S(1)}, f32[576,30]{0,1:T(8,128)}, u32[]{:S(2)}) copy-start(f32[576,30]{0,1:T(8,128)} %param.49) | copy-start | bytes 207364
  401.7 6.2 %copy-start.24 = (f32[576,30]{0,1:T(8,128)S(1)}, f32[576,30]{0,1:T(8,128)}, u32[]{:S(2)}) copy-start(f32[576,30]{0,1:T(8,128)} %param.50) | copy-start | bytes 207364
  401.7 6.9 %copy-start.28 = (f32[3,576]{1,0:T(4,128)S(1)}, f32[3,576]{1,0:T(4,128)}, u32[]{:S(2)}) copy-start(f32[3,576]{1,0:T(4,128)} %param.65) | copy-start | bytes 20740
